TPU v7x, 256 devices: a whole 4x4x8 slice. The times are simulated.
256 devices in a mesh: blk: 32 (over y, z_hi, x), head: 8 (over z_lo, core).
Axes of the slice: x: 4, y: 4, z: 8 (z_hi: 2, z_lo: 4; z = z_hi * 4 + z_lo), core: 2. Of those that a mesh axis runs over, the one named last changes fastest.
Arguments:
- queries: bfloat16 [4096, 3072], P(('blk', 'head')), may hold values from -32 to 32
- key_vectors: bfloat16 [4096, 3072], P(('blk', 'head')), may hold values from -9 to 9
- values: bfloat16 [4096, 3072], P(('blk', 'head')), may hold values from -6 to 6
- query_tangent: bfloat16 [4096, 3072], P(('blk', 'head')), may hold values from -6 to 6
- key_tangent: bfloat16 [4096, 3072], P(('blk', 'head')), may hold values from -6 to 6
- value_tangent: bfloat16 [4096, 3072], P(('blk', 'head')), may hold values from -6 to 6
- frame_index: int32 [4096], P('blk'), may hold values from 0 to 20, as said below
- valid_counts: int32 [32], P('blk'), may hold values from 32 to 128, as said below
Outputs:
- attended: bfloat16 [4096, 3072], P(('blk', 'head'))
- attended_tangent: bfloat16 [4096, 3072], P(('blk', 'head'))
Inputs may be any that keep to these rules, and one draw needn't show every extreme that they name: `frame_index`: never falls from one token to the next. `valid_counts`: every key block but the last is full (128 valid keys); the last holds at least 32.
All inputs are finite; a program needn't handle non-finite values.
Results may differ from a plain program's by a relative error of at most 0.033.
Values may be sent and summed in bfloat16 or wider, within the bound.
A program may use at most 128 MiB of HBM per device.

v0:
```python
import math

import jax
import jax.numpy as jnp
from jax import lax
from jax.sharding import PartitionSpec as P

HD = 128
FRAME_TOKENS = 3600
GRID_WIDTH = 80


def part_freqs(pair_count):
    indices = jnp.arange(pair_count, dtype=jnp.float32)
    return jnp.exp(-math.log(10000.0) * indices / pair_count)


def rotation(frames, token_ids):
    temporal = HD // 2 - 2 * (HD // 6)
    spatial = HD // 6
    height = (token_ids % FRAME_TOKENS // GRID_WIDTH).astype(jnp.float32)
    across = (token_ids % GRID_WIDTH).astype(jnp.float32)
    angles = jnp.concatenate(
        [
            frames.astype(jnp.float32)[:, None] * part_freqs(temporal)[None, :],
            height[:, None] * part_freqs(spatial)[None, :],
            across[:, None] * part_freqs(spatial)[None, :],
        ],
        axis=1,
    )
    cosine_table = jnp.cos(angles)
    sine_table = jnp.sin(angles)
    return (
        jnp.concatenate([cosine_table, cosine_table], axis=1),
        jnp.concatenate([-sine_table, sine_table], axis=1),
    )


def rotate(tensor, cosine_table, sine_table):
    widened = tensor.astype(jnp.float32)
    half_dim = HD // 2
    swapped = jnp.concatenate([widened[..., half_dim:], widened[..., :half_dim]], axis=-1)
    return (widened * cosine_table[:, None, :] + swapped * sine_table[:, None, :]).astype(
        jnp.bfloat16
    )


def heads_view(piece, heads_here):
    return piece.reshape(piece.shape[0], heads_here, HD)


def shards(
    queries,
    key_vectors,
    values,
    query_tangent,
    key_tangent,
    value_tangent,
    frame_index,
    valid_counts,
):
    arrived = (
        lax.all_to_all(queries, "head", split_axis=1, concat_axis=0, tiled=True),
        lax.all_to_all(key_vectors, "head", split_axis=1, concat_axis=0, tiled=True),
        lax.all_to_all(values, "head", split_axis=1, concat_axis=0, tiled=True),
        lax.all_to_all(query_tangent, "head", split_axis=1, concat_axis=0, tiled=True),
        lax.all_to_all(key_tangent, "head", split_axis=1, concat_axis=0, tiled=True),
        lax.all_to_all(value_tangent, "head", split_axis=1, concat_axis=0, tiled=True),
    )
    rows_here = arrived[0].shape[0]
    feature_width = arrived[0].shape[1]
    heads_here = feature_width // HD
    token_ids = lax.axis_index("blk") * rows_here + jnp.arange(rows_here, dtype=jnp.int32)
    cosine_table, sine_table = rotation(frame_index, token_ids)
    query_rot = rotate(heads_view(arrived[0], heads_here), cosine_table, sine_table)
    key_rot = rotate(heads_view(arrived[1], heads_here), cosine_table, sine_table).reshape(
        rows_here, feature_width
    )
    qtan_rot = rotate(heads_view(arrived[3], heads_here), cosine_table, sine_table)
    ktan_rot = rotate(heads_view(arrived[4], heads_here), cosine_table, sine_table).reshape(
        rows_here, feature_width
    )
    value_rows = arrived[2]
    vtan_rows = arrived[5]
    valid_rows = (jnp.arange(rows_here, dtype=jnp.int32) < valid_counts[0]).astype(jnp.int32)
    score_scale = 1.0 / math.sqrt(HD)

    def scores_of(key_piece, valid_piece):
        raw_scores = (
            jnp.einsum(
                "ihd,jhd->ihj",
                query_rot,
                heads_view(key_piece, heads_here),
                preferred_element_type=jnp.float32,
            )
            * score_scale
        )
        return jnp.where(valid_piece[None, None, :] > 0, raw_scores, -jnp.inf)

    def weighted_sum(weight_piece, value_piece):
        return jnp.einsum(
            "ihj,jhd->ihd",
            weight_piece,
            heads_view(value_piece, heads_here),
            preferred_element_type=jnp.float32,
        )

    start_max = jnp.full((rows_here, heads_here), -jnp.inf, jnp.float32)
    zero_rows = jnp.zeros((rows_here, heads_here), jnp.float32)
    zero_vectors = jnp.zeros((rows_here, heads_here, HD), jnp.float32)
    weight_total = zero_rows
    primal_acc = zero_vectors
    key_piece = lax.all_gather(key_rot, "blk", axis=0, tiled=True)
    value_piece = lax.all_gather(value_rows, "blk", axis=0, tiled=True)
    valid_piece = lax.all_gather(valid_rows, "blk", axis=0, tiled=True)
    scores = scores_of(key_piece, valid_piece)
    new_max = jnp.max(scores, axis=2)
    rescale = jnp.exp(start_max - new_max)
    weights = jnp.exp(scores - new_max[:, :, None])
    weight_total = weight_total * rescale + jnp.sum(weights, axis=2)
    primal_acc = primal_acc * rescale[:, :, None] + weighted_sum(
        weights.astype(jnp.bfloat16), value_piece
    )
    final_max, weight_total, primal_acc = (new_max, weight_total, primal_acc)
    key_piece = lax.all_gather(key_rot, "blk", axis=0, tiled=True)
    value_piece = lax.all_gather(value_rows, "blk", axis=0, tiled=True)
    ktan_piece = lax.all_gather(ktan_rot, "blk", axis=0, tiled=True)
    vtan_piece = lax.all_gather(vtan_rows, "blk", axis=0, tiled=True)
    valid_piece = lax.all_gather(valid_rows, "blk", axis=0, tiled=True)
    weights = jnp.exp(scores_of(key_piece, valid_piece) - final_max[:, :, None])
    first_term = jnp.einsum(
        "ihd,jhd->ihj",
        qtan_rot,
        heads_view(key_piece, heads_here),
        preferred_element_type=jnp.float32,
    )
    second_term = jnp.einsum(
        "ihd,jhd->ihj",
        query_rot,
        heads_view(ktan_piece, heads_here),
        preferred_element_type=jnp.float32,
    )
    weighted = weights * ((first_term + second_term) * score_scale)
    slope_sum = jnp.sum(weighted, axis=2)
    tangent_acc = weighted_sum(weighted.astype(jnp.bfloat16), value_piece) + weighted_sum(
        weights.astype(jnp.bfloat16), vtan_piece
    )
    slope_sum, tangent_acc = (slope_sum, tangent_acc)
    attended_full = primal_acc / weight_total[:, :, None]
    mean_slope = slope_sum / weight_total
    tangent_full = tangent_acc / weight_total[:, :, None] - mean_slope[:, :, None] * attended_full
    attended_low = attended_full.reshape(rows_here, feature_width).astype(jnp.bfloat16)
    tangent_low = tangent_full.reshape(rows_here, feature_width).astype(jnp.bfloat16)
    attended, attended_tangent = (
        lax.all_to_all(attended_low, "head", split_axis=0, concat_axis=1, tiled=True),
        lax.all_to_all(tangent_low, "head", split_axis=0, concat_axis=1, tiled=True),
    )
    return (attended, attended_tangent)


def solution(mesh):
    return jax.shard_map(
        shards,
        mesh=mesh,
        in_specs=(
            P(("blk", "head"), None),
            P(("blk", "head"), None),
            P(("blk", "head"), None),
            P(("blk", "head"), None),
            P(("blk", "head"), None),
            P(("blk", "head"), None),
            P("blk"),
            P("blk"),
        ),
        out_specs=(P(("blk", "head"), None), P(("blk", "head"), None)),
        check_vma=False,
    )
```

profile of v0, /device:TPU:1, one launch (start us, length us, event | category | flops | bytes accessed | tf_op | source)
XLA Modules:
  0.0 492.3 jit_solution(6042321685864870359)
XLA Ops:
  7.2 1.5 copy.155
  8.7 7.4 %all-to-all-start.5 = ((bf16[16,8,384]{2,0,1:T(8,128)(2,1)}), bf16[16,8,384]{2,0,1:T(8,128)(2,1)S(1)}, u32[]{:S(2)}, u32[]{:S(2)}) async-start(bf16[16,8,384]{2,0,1:T(8,128)(2,1)} %bitcast.105), calls=%async_computation.5 | async-start | bytes 196608 | tf_op jit(solution)/shard_map/all_to_all | solution.py:67
  16.8 1.5 copy.159
  18.4 1.5 copy.158
  20.4 1.2 all-to-all-done.5
  21.6 4.1 all-to-all-start
  26.3 4.9 %all-to-all-done = bf16[16,8,384]{2,0,1:T(8,128)(2,1)S(1)} async-done(((bf16[16,8,384]{2,0,1:T(8,128)(2,1)}), bf16[16,8,384]{2,0,1:T(8,128)(2,1)S(1)}, u32[]{:S(2)}, u32[]{:S(2)}) %all-to-all-start) | async-done | bytes 98336 | tf_op jit(solution)/shard_map/all_to_all | solution.py:64
  31.2 4.1 all-to-all-start.1
  35.9 4.9 all-to-all-done.1
  42.1 9.4 %all_to_all.122 = bf16[16,8,384]{2,0,1:T(8,128)(2,1)} all-to-all(bf16[16,8,384]{2,0,1:T(8,128)(2,1)S(1)} %bitcast.126), channel_id=1, replica_groups=mesh['blk'=32,'head'=8] {'head'}, dimensions={1} | all-to-all | bytes 196608 | tf_op jit(solution)/shard_map/all_to_all | solution.py:68
  52.5 9.6 %all_to_all.123 = bf16[16,8,384]{2,0,1:T(8,128)(2,1)} all-to-all(bf16[16,8,384]{2,0,1:T(8,128)(2,1)S(1)} %bitcast.127), channel_id=1, replica_groups=mesh['blk'=32,'head'=8] {'head'}, dimensions={1} | all-to-all | bytes 196608 | tf_op jit(solution)/shard_map/all_to_all | solution.py:65
  62.8 4.5 all-to-all-start.4
  68.0 104.1 %all-gather = s32[32,1,128]{2,1,0:T(1,128)S(1)} all-gather(s32[1,1,128]{2,1,0:T(1,128)S(1)} %fusion.38), channel_id=1, replica_groups=mesh['blk'=32,'head'=8] {'blk'}, dimensions={0}, use_global_device_ids=true | all-gather | bytes 16896 | tf_op jit(solution)/shard_map/all_gather | solution.py:115
  173.0 3.2 copy.91
  176.2 65.2 %all-gather.12.cloned.1.call-done = bf16[4096,384]{1,0:T(8,128)(2,1)} async-done(((bf16[128,384]{1,0:T(8,128)(2,1)}), bf16[4096,384]{1,0:T(8,128)(2,1)}) %all-gather.12.cloned.1.call-update) | async-done | bytes 3145744 | tf_op jit(solution)/shard_map/all_gather | solution.py:128
  241.4 4.8 copy.119
  246.2 2.4 bitcast_reduce_fusion
  248.7 0.8 fusion.1
  249.5 2.3 copy-done
  251.8 1.0 copy-done.2
  252.8 3.9 fusion.32
  256.7 98.6 %all-gather.10.cloned.1.call-done = bf16[4096,384]{0,1:T(8,128)(2,1)} async-done(((bf16[128,384]{0,1:T(8,128)(2,1)}), bf16[4096,384]{0,1:T(8,128)(2,1)}) %all-gather.10.cloned.1.call-update) | async-done | bytes 3145744 | tf_op jit(solution)/shard_map/all_gather | solution.py:127
  355.3 9.7 %fusion.52 = (f32[128,3]{0,1:T(4,128)S(1)}, bf16[128,3,4096]{0,2,1:T(8,128)(2,1)}) fusion(f32[3,4096,128]{2,1,0:T(8,128)} %fusion.32, bf16[4096,3,128]{0,2,1:T(8,128)(2,1)} %bitcast.118, bf16[128,3,128]{0,2,1:T(8,128)(2,1)S(1)} %get-tuple-element.17, f32[128,3]{0,1:T(4,128)S(1)} %get-tuple-element.23, f32[3,4096,128]{2,1,0:T(8,128)} %copy-done), kind=kOutput, calls=%fused_computation.73 | convolution fusion | flops 412089984 | bytes 18975744 | tf_op jit(solution)/shard_map/ihd,jhd->ihj/dot_general | solution.py:137
  365.0 1.6 fusion.22
  366.6 88.3 %all-gather.8.cloned.1.call-done = bf16[4096,384]{1,0:T(8,128)(2,1)} async-done(((bf16[128,384]{1,0:T(8,128)(2,1)}), bf16[4096,384]{1,0:T(8,128)(2,1)}) %all-gather.8.cloned.1.call-update) | async-done | bytes 3145744 | tf_op jit(solution)/shard_map/all_gather | solution.py:114
  454.9 3.2 copy.99
  458.1 4.3 fusion.53
  462.5 1.1 fusion.19
  464.4 5.5 %all-to-all-start.7 = ((bf16[8,16,384]{2,1,0:T(8,128)(2,1)}), bf16[8,16,384]{2,1,0:T(8,128)(2,1)S(1)}, u32[]{:S(2)}, u32[]{:S(2)}) async-start(bf16[8,16,384]{2,1,0:T(8,128)(2,1)} %convert_element_type.134), calls=%async_computation.7 | async-start | bytes 196608 | tf_op jit(solution)/shard_map/all_to_all | solution.py:156
  470.8 4.7 all-to-all-done.7
  475.5 4.1 all-to-all-start.3
  480.2 4.9 all-to-all-done.3
  (83 shorter events, 8.9 us)
Async XLA Ops:
  8.7 12.9 %all-to-all-start.5 = ((bf16[16,8,384]{2,0,1:T(8,128)(2,1)}), bf16[16,8,384]{2,0,1:T(8,128)(2,1)S(1)}, u32[]{:S(2)}, u32[]{:S(2)}) async-start(bf16[16,8,384]{2,0,1:T(8,128)(2,1)} %bitcast.105), calls=%async_computation.5 | async-start | bytes 196608 | tf_op jit(solution)/shard_map/all_to_all | solution.py:67
  20.4 20.8 %copy-start.5 = (f32[128,128]{0,1:T(8,128)}, f32[128,128]{0,1:T(8,128)S(1)}, u32[]{:S(2)}) copy-start(f32[128,128]{0,1:T(8,128)S(1)} %pad_maximum_fusion.1) | copy-start | bytes 196612
  21.6 9.6 %all-to-all-start = ((bf16[16,8,384]{2,0,1:T(8,128)(2,1)}), bf16[16,8,384]{2,0,1:T(8,128)(2,1)S(1)}, u32[]{:S(2)}, u32[]{:S(2)}) async-start(bf16[16,8,384]{2,0,1:T(8,128)(2,1)} %bitcast.109), calls=%async_computation | async-start | bytes 196608 | tf_op jit(solution)/shard_map/all_to_all | solution.py:64
  31.2 9.6 %all-to-all-start.1 = ((bf16[16,8,384]{2,0,1:T(8,128)(2,1)}), bf16[16,8,384]{2,0,1:T(8,128)(2,1)S(1)}, u32[]{:S(2)}, u32[]{:S(2)}) async-start(bf16[16,8,384]{2,0,1:T(8,128)(2,1)} %bitcast.108), calls=%async_computation.1 | async-start | bytes 196608 | tf_op jit(solution)/shard_map/all_to_all | solution.py:63
  35.4 137.7 %all-gather.6.cloned.1.call-start = ((), (), s32[]{:S(2)}) async-start(), calls=%async_computation.8 | async-start | bytes 3244032 | tf_op jit(solution)/shard_map/all_gather | solution.py:113
  35.4 6.7 %copy-start.9 = (bf16[16,3072]{1,0:T(8,128)(2,1)S(1)}, bf16[16,3072]{1,0:T(8,128)(2,1)}, u32[]{:S(2)}) copy-start(bf16[16,3072]{1,0:T(8,128)(2,1)} %param.13) | copy-start | bytes 294916
  35.7 16.8 %copy-start.10 = (bf16[16,3072]{1,0:T(8,128)(2,1)S(1)}, bf16[16,3072]{1,0:T(8,128)(2,1)}, u32[]{:S(2)}) copy-start(bf16[16,3072]{1,0:T(8,128)(2,1)} %param.10) | copy-start | bytes 294916
  35.9 26.2 %copy-start.11 = (bf16[16,3072]{1,0:T(8,128)(2,1)S(1)}, bf16[16,3072]{1,0:T(8,128)(2,1)}, u32[]{:S(2)}) copy-start(bf16[16,3072]{1,0:T(8,128)(2,1)} %param.11) | copy-start | bytes 294916
  42.0 199.4 %all-gather.12.cloned.1.call-start = ((), (), s32[]{:S(2)}) async-start(), calls=%async_computation.11 | async-start | bytes 3244032 | tf_op jit(solution)/shard_map/all_gather | solution.py:128
  51.6 303.7 %all-gather.10.cloned.1.call-start = ((), (), s32[]{:S(2)}) async-start(), calls=%async_computation.10 | async-start | bytes 3244032 | tf_op jit(solution)/shard_map/all_gather | solution.py:127
  52.4 402.5 %all-gather.8.cloned.1.call-start = ((), (), s32[]{:S(2)}) async-start(), calls=%async_computation.9 | async-start | bytes 3244032 | tf_op jit(solution)/shard_map/all_gather | solution.py:114
  62.8 109.3 %all-to-all-start.4 = ((bf16[16,8,384]{2,0,1:T(8,128)(2,1)}), bf16[16,8,384]{2,0,1:T(8,128)(2,1)S(1)}, u32[]{:S(2)}, u32[]{:S(2)}) async-start(bf16[16,8,384]{2,0,1:T(8,128)(2,1)} %bitcast.106), calls=%async_computation.4 | async-start | bytes 196608 | tf_op jit(solution)/shard_map/all_to_all | solution.py:66
  176.2 70.0 %copy-start.1 = (bf16[4096,384]{0,1:T(8,128)(2,1)}, bf16[4096,384]{0,1:T(8,128)(2,1)S(1)}, u32[]{:S(2)}) copy-start(bf16[4096,384]{0,1:T(8,128)(2,1)S(1)} %copy.91) | copy-start | bytes 9437188
  248.6 3.2 copy-start
  248.6 4.2 copy-start.2
  248.6 4.2 copy-start.6
  248.6 4.2 copy-start.7
  248.7 4.1 copy-start.8
  252.8 112.2 %slice-start = ((s8[6291456]{0:T(1024)(128)(4,1)}), s8[2097152]{0:T(1024)(128)(4,1)S(1)}, s32[]{:S(2)}) async-start(s8[6291456]{0:T(1024)(128)(4,1)} %bitcast.111), calls=%async_computation.12 | async-start | bytes 4194304
  355.3 9.7 %slice-start.1 = ((s8[6291456]{0:T(1024)(128)(4,1)}), s8[4194304]{0:T(1024)(128)(4,1)S(1)}, s32[]{:S(2)}) async-start(s8[6291456]{0:T(1024)(128)(4,1)} %bitcast.111), calls=%async_computation.13 | async-start | bytes 8388608
  355.3 9.7 %copy-start.3 = (bf16[4096,384]{0,1:T(8,128)(2,1)S(1)}, bf16[4096,384]{0,1:T(8,128)(2,1)}, u32[]{:S(2)}) copy-start(bf16[4096,384]{0,1:T(8,128)(2,1)} %copy.119) | copy-start | bytes 9437188
  458.1 4.3 copy-start.4
  464.4 11.0 %all-to-all-start.7 = ((bf16[8,16,384]{2,1,0:T(8,128)(2,1)}), bf16[8,16,384]{2,1,0:T(8,128)(2,1)S(1)}, u32[]{:S(2)}, u32[]{:S(2)}) async-start(bf16[8,16,384]{2,1,0:T(8,128)(2,1)} %convert_element_type.134), calls=%async_computation.7 | async-start | bytes 196608 | tf_op jit(solution)/shard_map/all_to_all | solution.py:156
  475.5 9.6 %all-to-all-start.3 = ((bf16[8,16,384]{2,1,0:T(8,128)(2,1)}), bf16[8,16,384]{2,1,0:T(8,128)(2,1)S(1)}, u32[]{:S(2)}, u32[]{:S(2)}) async-start(bf16[8,16,384]{2,1,0:T(8,128)(2,1)} %convert_element_type.121), calls=%async_computation.3 | async-start | bytes 196608 | tf_op jit(solution)/shard_map/all_to_all | solution.py:155
Sparse Core Ops, SparseCore 0:
  42.2 100.8 all-gather.5
  146.5 94.8 all-gather.11
  244.6 110.6 all-gather.9
  358.5 96.3 all-gather.7
where the time goes:
time: 493 us; the launch traced here: 492 us
  waiting for transfers between devices  273 us (55%)
  blocking collectives  123 us (25%)
  starting transfers between devices  29.9 us (6%)
  local copies, waits for them, and re-layouts  25.3 us (5%)
  matrix products  23 us (5%)
  between operations  14.8 us (3%)
    all_gather x1, blocking collectives, shards(): valid_piece = lax.all_gather(valid_rows, 'blk', axis=0, tiled=True)  104 us
    all_gather x1, waiting for transfers between devices, shards(): ktan_piece = lax.all_gather(ktan_rot, 'blk', axis=0, tiled=True)  98.6 us
    all_gather x1, waiting for transfers between devices, shards(): value_piece = lax.all_gather(value_rows, 'blk', axis=0, tiled=True)  88.3 us
    all_gather x1, waiting for transfers between devices, shards(): vtan_piece = lax.all_gather(vtan_rows, 'blk', axis=0, tiled=True)  65.2 us
  transfers between devices with their start and end apart: 10, of which 8 were waited for; matrix products, arithmetic and copies ran while one was open for 7% of the time, Pallas kernels for 0%

commit v1 on v0

v1 whole, which is shorter than its diff:
```python
import math

import jax
import jax.numpy as jnp
from jax import lax
from jax.experimental import pallas as pl
from jax.experimental.pallas import tpu as pltpu
from jax.sharding import PartitionSpec as P

HD = 128
FRAME_TOKENS = 3600
GRID_WIDTH = 80
ROWS = 16

X, Y, ZH, ZL, C = 4, 4, 2, 4, 2
J = 3

MARK = 16384.0
MARK_SUM = 1.0e5
LOW = -1.0e30

K, KT, Q, QT, V, VT = range(6)
GROUPS = ((0, 1), (1, 3), (4, 2))
RING = (K, KT, V, VT)


def part_freqs(pair_count):
    indices = jnp.arange(pair_count, dtype=jnp.float32)
    return jnp.exp(-math.log(10000.0) * indices / pair_count)


def rotation(frames, token_ids):
    temporal = HD // 2 - 2 * (HD // 6)
    spatial = HD // 6
    height = (token_ids % FRAME_TOKENS // GRID_WIDTH).astype(jnp.float32)
    across = (token_ids % GRID_WIDTH).astype(jnp.float32)
    angles = jnp.concatenate(
        [
            frames.astype(jnp.float32)[:, None] * part_freqs(temporal)[None, :],
            height[:, None] * part_freqs(spatial)[None, :],
            across[:, None] * part_freqs(spatial)[None, :],
        ],
        axis=1,
    )
    cosine_table = jnp.cos(angles)
    sine_table = jnp.sin(angles)
    return (
        jnp.concatenate([cosine_table, cosine_table], axis=1),
        jnp.concatenate([-sine_table, sine_table], axis=1),
    )


def device(x, y, z, c):
    return (y * (ZH * X) + lax.div(z, ZL) * X + x, lax.rem(z, ZL) * C + c)


def nt_dot(a, b):
    return lax.dot_general(a, b, (((1,), (1,)), ((), ())), preferred_element_type=jnp.float32)


def nn_dot(a, b):
    return jnp.dot(a, b, preferred_element_type=jnp.float32)


def kernel(
    q_ref, k_ref, v_ref, qt_ref, kt_ref, vt_ref, cos_ref, sin_ref, valid_ref,
    o_ref, ot_ref,
    send, kv, s_ref, p_ref, w_ref, acc_p, acc_w, mx, lsum, gsum, outsend, outland,
    dsem, rsem, ssem, dsend, rsend, bsend, osem, osend,
):
    Z = ZH * ZL
    heads = Z * J
    span = Z * ROWS
    chunks = X * C
    half = Y // 2
    keys = Y * span
    scale = 1.0 / math.sqrt(HD)
    scale2 = scale * math.log2(math.e)

    blk = lax.axis_index("blk")
    hd = lax.axis_index("head")
    x = lax.rem(blk, X)
    y = lax.div(blk, ZH * X)
    z = lax.rem(lax.div(blk, X), ZH) * ZL + lax.div(hd, C)
    c = lax.rem(hd, C)
    right = device(lax.rem(x + 1, X), y, z, c)
    left = device(lax.rem(x + X - 1, X), y, z, c)
    sib = device(x, y, z, 1 - c)
    own = (x * C + c) * Y
    computes = y < J

    barrier = pltpu.get_barrier_semaphore()

    def greet(i, carry):
        gy = lax.div(i, Z)
        gz = lax.rem(i, Z)

        @pl.when(jnp.logical_or(gy != y, gz != z))
        def _():
            pl.semaphore_signal(barrier, inc=1, device_id=device(x, gy, gz, c))

        return carry

    lax.fori_loop(0, Y * Z, greet, 0)
    for other in (right, left, sib):
        pl.semaphore_signal(barrier, inc=1, device_id=other)

    cosine = cos_ref[...]
    sine = sin_ref[...]
    valid = valid_ref[...] > 0.0

    def rotate(ref, slot, marked):
        for h in range(heads):
            wide = ref[:, h * HD : (h + 1) * HD].astype(jnp.float32)
            turned = wide * cosine + pltpu.roll(wide, HD // 2, 1) * sine
            if marked:
                turned = jnp.where(valid, turned, MARK)
            send[h, slot] = turned.astype(jnp.bfloat16)

    def place(ref, slot):
        for h in range(heads):
            send[h, slot] = ref[:, h * HD : (h + 1) * HD]

    def direct(g):
        first, count = GROUPS[g]

        def step(i, carry):
            m = lax.div(i + 1, 2)
            tz = lax.rem(z + jnp.where(lax.rem(i, 2) == 1, m, Z - m), Z)
            for j in range(J):
                src = send.at[tz * J + j, pl.ds(first, count)]
                dst = kv.at[pl.ds(first, count), own + y, pl.ds(z * ROWS, ROWS)]
                here = jnp.logical_and(tz == z, y == j)

                @pl.when(here)
                def _():
                    pltpu.make_async_copy(src, dst, dsem.at[g]).start()

                @pl.when(jnp.logical_not(here))
                def _():
                    pltpu.make_async_remote_copy(
                        src_ref=src, dst_ref=dst, send_sem=dsend.at[g], recv_sem=dsem.at[g],
                        device_id=device(x, j, tz, c),
                    ).start()

            return carry

        lax.fori_loop(0, Z, step, 0)

    def wait_direct(g):
        first, count = GROUPS[g]
        region = kv.at[pl.ds(first, count), pl.ds(own, Y)]
        pltpu.make_async_copy(region, region, dsem.at[g]).wait()

    def region(a, sx, sc, u):
        return kv.at[a, pl.ds((sx * C + sc) * Y + u * half, half)]

    def ring_send(a, part, to, event):
        n = RING.index(a)
        pltpu.make_async_remote_copy(
            src_ref=part, dst_ref=part, send_sem=rsend.at[n], recv_sem=rsem.at[n, event],
            device_id=to,
        ).start()

    def sib_send(a, part):
        n = RING.index(a)
        pltpu.make_async_remote_copy(
            src_ref=part, dst_ref=part, send_sem=bsend.at[n], recv_sem=ssem.at[n],
            device_id=sib,
        ).start()

    def start_own(a):
        first, second = region(a, x, c, 0), region(a, x, c, 1)
        ring_send(a, first, right, 2)
        ring_send(a, second, left, 3)
        ring_send(a, second, right, 4)
        ring_send(a, first, left, 5)
        sib_send(a, first)
        sib_send(a, second)

    def event(a, i):
        n = RING.index(a)
        far = jnp.where(i >= 6, 2, 1)
        from_left = lax.rem(i, 2) == 0
        sx = lax.rem(jnp.where(from_left, x + X - far, x + far), X)
        u = jnp.where(from_left, jnp.where(i == 4, 1, 0), jnp.where(i == 5, 0, 1))
        part = region(a, sx, c, u)
        pltpu.make_async_copy(part, part, rsem.at[n, i]).wait()

        @pl.when(i == 2)
        def _():
            ring_send(a, part, right, 6)

        @pl.when(i == 3)
        def _():
            ring_send(a, part, left, 7)

        sib_send(a, part)

    def wait_sib(a):
        part = kv.at[a, pl.ds(0, chunks * Y // 2)]
        pltpu.make_async_copy(part, part, ssem.at[RING.index(a)]).wait()

    def queries_of(a):
        return kv[a, pl.ds(own, Y)].reshape(keys, HD)

    def chunk(a, i):
        return kv[a, pl.ds(i * Y, Y)].reshape(keys, HD)

    def lanes(op, total, array):
        for t in range(array.shape[1] // HD):
            total = op(total, array[:, t * HD : (t + 1) * HD])
        return total

    def scores(i):
        s = nt_dot(queries_of(Q), chunk(K, i))
        tail = keys - span
        marks = nt_dot(jnp.ones((8, HD), jnp.bfloat16), kv[K, i * Y + Y - 1])[0:1]
        last = jnp.where(marks > MARK_SUM, LOW, s[:, tail:])
        s = jnp.concatenate([s[:, :tail], last], axis=1)
        s_ref[i] = s
        mx[...] = lanes(jnp.maximum, mx[...], s)

    def weights(i):
        top = jnp.concatenate([mx[...]] * (keys // HD), axis=1)
        p = jnp.exp2(s_ref[i] * scale2 - top)
        g = nt_dot(
            jnp.concatenate([queries_of(QT), queries_of(Q)], axis=1),
            jnp.concatenate([chunk(K, i), chunk(KT, i)], axis=1),
        )
        w = p * g
        lsum[...] = lanes(jnp.add, lsum[...], p)
        gsum[...] = lanes(jnp.add, gsum[...], w)
        p_ref[i] = p.astype(jnp.bfloat16)
        w_ref[i] = w.astype(jnp.bfloat16)

    def slope_values(i):
        acc_w[...] += nn_dot(w_ref[i], chunk(V, i))

    def weight_values(i):
        acc_p[...] += nn_dot(p_ref[i], jnp.concatenate([chunk(V, i), chunk(VT, i)], axis=1))

    rotate(k_ref, K, True)
    pl.semaphore_wait(barrier, Y * Z - 1 + 3)
    direct(0)
    rotate(kt_ref, KT, False)
    rotate(q_ref, Q, False)
    rotate(qt_ref, QT, False)
    direct(1)
    place(v_ref, V)
    place(vt_ref, VT)
    direct(2)

    @pl.when(computes)
    def _():
        mx[...] = jnp.full_like(mx, LOW)
        lsum[...] = jnp.zeros_like(lsum)
        gsum[...] = jnp.zeros_like(gsum)
        acc_p[...] = jnp.zeros_like(acc_p)
        acc_w[...] = jnp.zeros_like(acc_w)

        def phase(a, work, following):
            def step(i, carry):
                @pl.when(i >= 2)
                def _():
                    event(a, i)

                if following is not None:

                    @pl.when(i == 4)
                    def _():
                        following()

                if work is not None:
                    work(i)
                return carry

            lax.fori_loop(0, 8, step, 0)
            wait_sib(a)

        def begin(g, a):
            wait_direct(g)
            start_own(a)

        begin(0, K)
        phase(K, None, lambda: begin(1, KT))
        phase(KT, scores, lambda: begin(2, V))
        mx[...] = jnp.broadcast_to(
            jnp.max(mx[...], axis=1, keepdims=True) * scale2, mx.shape
        )
        phase(V, weights, lambda: start_own(VT))
        phase(VT, slope_values, None)

        def tail(i, carry):
            weight_values(i)
            return carry

        lax.fori_loop(0, chunks, tail, 0)

        inverse = 1.0 / jnp.sum(lsum[...], axis=1, keepdims=True)
        slope = jnp.sum(gsum[...], axis=1, keepdims=True) * inverse * scale
        attended = acc_p[:, :HD] * inverse
        tangent = (acc_w[...] * scale + acc_p[:, HD:]) * inverse - slope * attended
        outsend[:, 0] = attended.astype(jnp.bfloat16).reshape(Y * Z, ROWS, HD)
        outsend[:, 1] = tangent.astype(jnp.bfloat16).reshape(Y * Z, ROWS, HD)

        def give(i, carry):
            m = lax.div(i + 1, 2)
            tz = lax.rem(z + jnp.where(lax.rem(i, 2) == 1, m, Z - m), Z)
            for ty in range(Y):
                src = outsend.at[ty * Z + tz]
                dst = outland.at[z * J + y]
                here = jnp.logical_and(tz == z, y == ty)

                @pl.when(here)
                def _():
                    pltpu.make_async_copy(src, dst, osem).start()

                @pl.when(jnp.logical_not(here))
                def _():
                    pltpu.make_async_remote_copy(
                        src_ref=src, dst_ref=dst, send_sem=osend, recv_sem=osem,
                        device_id=device(x, ty, tz, c),
                    ).start()

            return carry

        lax.fori_loop(0, Z, give, 0)

    pltpu.make_async_copy(outland, outland, osem).wait()
    for h in range(heads):
        o_ref[:, h * HD : (h + 1) * HD] = outland[h, 0]
        ot_ref[:, h * HD : (h + 1) * HD] = outland[h, 1]

    def sent(g, count):
        first, arrays = GROUPS[g]
        part = send.at[pl.ds(0, count), pl.ds(first, arrays)]
        pltpu.make_async_copy(part, part, dsend.at[g]).wait()

    @pl.when(computes)
    def _():
        for g in range(3):
            sent(g, heads - 1)
        for n in range(4):
            part = kv.at[0, pl.ds(0, 6 * half)]
            pltpu.make_async_copy(part, part, rsend.at[n]).wait()
            part = kv.at[0, pl.ds(0, 8 * half)]
            pltpu.make_async_copy(part, part, bsend.at[n]).wait()
        part = outsend.at[pl.ds(0, Y * Z - 1)]
        pltpu.make_async_copy(part, part, osend).wait()

    @pl.when(jnp.logical_not(computes))
    def _():
        for g in range(3):
            sent(g, heads)


def shards(queries, key_vectors, values, query_tangent, key_tangent, value_tangent,
           frame_index, valid_counts):
    Z = ZH * ZL
    heads = Z * J
    span = Z * ROWS
    rows = Y * span
    chunks = X * C
    blk = lax.axis_index("blk")
    hd = lax.axis_index("head")
    inner = hd * ROWS + jnp.arange(ROWS, dtype=jnp.int32)
    token_ids = blk * (ROWS * ZL * C) + inner
    frames = lax.dynamic_slice(frame_index, (hd * ROWS,), (ROWS,))
    cosine_table, sine_table = rotation(frames, token_ids)
    valid = jnp.broadcast_to((inner < valid_counts[0]).astype(jnp.float32)[:, None], (ROWS, HD))

    vmem = pl.BlockSpec(memory_space=pltpu.VMEM)
    out = jax.ShapeDtypeStruct((ROWS, heads * HD), jnp.bfloat16)
    return pl.pallas_call(
        kernel,
        out_shape=(out, out),
        in_specs=[vmem] * 9,
        out_specs=(vmem, vmem),
        scratch_shapes=[
            pltpu.VMEM((heads, 6, ROWS, HD), jnp.bfloat16),
            pltpu.VMEM((6, chunks * Y, span, HD), jnp.bfloat16),
            pltpu.VMEM((chunks, rows, rows), jnp.float32),
            pltpu.VMEM((chunks, rows, rows), jnp.bfloat16),
            pltpu.VMEM((chunks, rows, rows), jnp.bfloat16),
            pltpu.VMEM((rows, 2 * HD), jnp.float32),
            pltpu.VMEM((rows, HD), jnp.float32),
            pltpu.VMEM((rows, HD), jnp.float32),
            pltpu.VMEM((rows, HD), jnp.float32),
            pltpu.VMEM((rows, HD), jnp.float32),
            pltpu.VMEM((Y * Z, 2, ROWS, HD), jnp.bfloat16),
            pltpu.VMEM((heads, 2, ROWS, HD), jnp.bfloat16),
            pltpu.SemaphoreType.DMA((3,)),
            pltpu.SemaphoreType.DMA((4, 8)),
            pltpu.SemaphoreType.DMA((4,)),
            pltpu.SemaphoreType.DMA((3,)),
            pltpu.SemaphoreType.DMA((4,)),
            pltpu.SemaphoreType.DMA((4,)),
            pltpu.SemaphoreType.DMA,
            pltpu.SemaphoreType.DMA,
        ],
        compiler_params=pltpu.CompilerParams(
            collective_id=0, has_side_effects=True, vmem_limit_bytes=52 * 1024 * 1024
        ),
    )(queries, key_vectors, values, query_tangent, key_tangent, value_tangent,
      cosine_table, sine_table, valid)


def solution(mesh):
    tokens = P(("blk", "head"), None)
    return jax.shard_map(
        shards,
        mesh=mesh,
        in_specs=(tokens,) * 6 + (P("blk"), P("blk")),
        out_specs=(tokens, tokens),
        check_vma=False,
    )
```

time: 493 us -> 68.3 us (0.14)
  waiting for transfers between devices: 273 us -> 0 us
  blocking collectives: 123 us -> 0 us
  Pallas kernels: 0 us -> 59.6 us
  starting transfers between devices: 29.9 us -> 0 us
  matrix products: 23 us -> 0 us
  local copies, waits for them, and re-layouts: 25.3 us -> 5.82 us
  between operations: 14.8 us -> 1.36 us
    all_gather x4 -> x0, waiting for transfers between devices: 252 us -> none  [the longest x1 98.6 us: shards(): ktan_piece = lax.all_gather(ktan_rot, 'blk', axis=0, tiled=True)]
    all_gather x1 -> x0, blocking collectives: 104 us -> none  [shards(): valid_piece = lax.all_gather(valid_rows, 'blk', axis=0, tiled=True)]
    pallas_call x0 -> x1, Pallas kernels: none -> 59.6 us  [shards(): pl.pallas_call(kernel, out_shape=(out, out), in_specs=[vmem] * 9, out_spe...]
    all_to_all x6 -> x0, starting transfers between devices: 29.8 us -> none  [the longest x1 7.4 us: shards(): lax.all_to_all(key_tangent, 'head', split_axis=1, concat_axis=0, tiled=True)]
    dot_general x6 -> x0, matrix products: 23 us -> none  [the longest x1 9.71 us: shards(): jnp.einsum('ihd,jhd->ihj', query_rot, heads_view(ktan_piece, heads_here),...]
    all_to_all x6 -> x0, waiting for transfers between devices: 20.6 us -> none  [the longest x1 4.94 us: shards(): lax.all_to_all(key_vectors, 'head', split_axis=1, concat_axis=0, tiled=True)]
    all_to_all x2 -> x0, blocking collectives: 19 us -> none  [the longest x1 9.63 us: shards(): lax.all_to_all(values, 'head', split_axis=1, concat_axis=0, tiled=True)]
    all_gather x3 -> x0, local copies, waits for them, and re-layouts: 11.1 us -> none  [the longest x1 4.77 us: shards(): vtan_piece = lax.all_gather(vtan_rows, 'blk', axis=0, tiled=True)]
  transfers between devices with their start and end apart: 10 -> 0, of which waited for: 8 -> 0; matrix products, arithmetic and copies ran while one was open for 7% -> 0% of each run, Pallas kernels for 0% -> 0%
where the time goes in v1:
time: 68.3 us; the launch traced here: 68 us
  Pallas kernels  59.6 us (87%)
  local copies, waits for them, and re-layouts  5.82 us (9%)
  between operations  1.36 us (2%)
  other arithmetic  1.21 us (2%)
    pallas_call x1, Pallas kernels, shards(): pl.pallas_call(kernel, out_shape=(out, out), in_specs=[vmem] * 9, out_spe...  59.6 us
    unnamed x14, local copies, waits for them, and re-layouts  5.75 us

profile of v1, /device:TPU:1, one launch (start us, length us, event | category | flops | bytes accessed | tf_op | source)
XLA Modules:
  0.0 68.0 jit_solution(17827041279243767106)
XLA Ops:
  0.6 0.0 copy-start
  1.3 0.7 %dynamic-slice_convert_fusion = f32[16]{0:T(128)S(1)} fusion(s32[128]{0:T(128)} %param.14, s32[]{:T(128)S(6)} %select_n.31), kind=kLoop, calls=%fused_computation.16 | loop fusion | flops 16 | bytes 132 | tf_op jit(solution)/shard_map/convert_element_type | solution.py:39
  2.1 0.1 broadcast_multiply_fusion.2
  2.2 0.1 broadcast_in_dim.2.valid_ref
  2.3 0.1 broadcast_multiply_fusion.1
  2.3 0.1 fusion.5
  2.5 0.1 pad_maximum_fusion.2.sin_ref
  2.5 0.1 pad_maximum_fusion.1.cos_ref
  2.6 0.0 copy-done
  2.6 0.0 copy-start.1
  2.6 0.9 %copy-done.1 = bf16[16,3072]{1,0:T(8,128)(2,1)S(1)} copy-done((bf16[16,3072]{1,0:T(8,128)(2,1)S(1)}, bf16[16,3072]{1,0:T(8,128)(2,1)}, u32[]{:S(2)}) %copy-start.1) | copy-done | bytes 98328
  3.5 0.0 copy-start.2
  3.5 0.9 %copy-done.2 = bf16[16,3072]{1,0:T(8,128)(2,1)S(1)} copy-done((bf16[16,3072]{1,0:T(8,128)(2,1)S(1)}, bf16[16,3072]{1,0:T(8,128)(2,1)}, u32[]{:S(2)}) %copy-start.2) | copy-done | bytes 98328
  4.4 0.0 copy-start.3
  4.4 0.9 %copy-done.3 = bf16[16,3072]{1,0:T(8,128)(2,1)S(1)} copy-done((bf16[16,3072]{1,0:T(8,128)(2,1)S(1)}, bf16[16,3072]{1,0:T(8,128)(2,1)}, u32[]{:S(2)}) %copy-start.3) | copy-done | bytes 98328
  5.3 0.0 copy-start.4
  5.3 0.9 %copy-done.4 = bf16[16,3072]{1,0:T(8,128)(2,1)S(1)} copy-done((bf16[16,3072]{1,0:T(8,128)(2,1)S(1)}, bf16[16,3072]{1,0:T(8,128)(2,1)}, u32[]{:S(2)}) %copy-start.4) | copy-done | bytes 98328
  6.2 0.0 copy-start.5
  6.2 0.9 %copy-done.5 = bf16[16,3072]{1,0:T(8,128)(2,1)S(1)} copy-done((bf16[16,3072]{1,0:T(8,128)(2,1)S(1)}, bf16[16,3072]{1,0:T(8,128)(2,1)}, u32[]{:S(2)}) %copy-start.5) | copy-done | bytes 98328
  7.1 59.6 %shard_map.95 = (bf16[16,3072]{1,0:T(8,128)(2,1)S(1)}, bf16[16,3072]{1,0:T(8,128)(2,1)S(1)}) custom-call(bf16[16,3072]{1,0:T(8,128)(2,1)S(1)} %copy-done, bf16[16,3072]{1,0:T(8,128)(2,1)S(1)} %copy-done.1, bf16[16,3072]{1,0:T(8,128)(2,1)S(1)} %copy-done.2, bf16[16,3072]{1,0:T(8,128)(2,1)S(1)} %copy-done.3, bf16[16,3072]{1,0:T(8,128)(2,1)S(1)} %copy-done.4, ...), custom_call_target="tpu_custom_call" | custom-call | tf_op jit(solution)/shard_map/pallas_call | solution.py:375
  66.7 0.6 copy.13
  67.3 0.6 copy.14
  (4 shorter events, 0.0 us)
Async XLA Ops:
  0.6 2.0 %copy-start = (bf16[16,3072]{1,0:T(8,128)(2,1)S(1)}, bf16[16,3072]{1,0:T(8,128)(2,1)}, u32[]{:S(2)}) copy-start(bf16[16,3072]{1,0:T(8,128)(2,1)} %q_ref.1) | copy-start | bytes 294916
  2.6 0.9 %copy-start.1 = (bf16[16,3072]{1,0:T(8,128)(2,1)S(1)}, bf16[16,3072]{1,0:T(8,128)(2,1)}, u32[]{:S(2)}) copy-start(bf16[16,3072]{1,0:T(8,128)(2,1)} %k_ref.1) | copy-start | bytes 294916
  3.5 0.9 %copy-start.2 = (bf16[16,3072]{1,0:T(8,128)(2,1)S(1)}, bf16[16,3072]{1,0:T(8,128)(2,1)}, u32[]{:S(2)}) copy-start(bf16[16,3072]{1,0:T(8,128)(2,1)} %v_ref.1) | copy-start | bytes 294916
  4.4 0.9 %copy-start.3 = (bf16[16,3072]{1,0:T(8,128)(2,1)S(1)}, bf16[16,3072]{1,0:T(8,128)(2,1)}, u32[]{:S(2)}) copy-start(bf16[16,3072]{1,0:T(8,128)(2,1)} %qt_ref.1) | copy-start | bytes 294916
  5.3 0.9 %copy-start.4 = (bf16[16,3072]{1,0:T(8,128)(2,1)S(1)}, bf16[16,3072]{1,0:T(8,128)(2,1)}, u32[]{:S(2)}) copy-start(bf16[16,3072]{1,0:T(8,128)(2,1)} %kt_ref.1) | copy-start | bytes 294916
  6.2 0.9 %copy-start.5 = (bf16[16,3072]{1,0:T(8,128)(2,1)S(1)}, bf16[16,3072]{1,0:T(8,128)(2,1)}, u32[]{:S(2)}) copy-start(bf16[16,3072]{1,0:T(8,128)(2,1)} %vt_ref.1) | copy-start | bytes 294916

commit v2 on v1

v2 whole, which is shorter than its diff:
```python
import math

import jax
import jax.numpy as jnp
from jax import lax
from jax.experimental import pallas as pl
from jax.experimental.pallas import tpu as pltpu
from jax.sharding import PartitionSpec as P

HD = 128
FRAME_TOKENS = 3600
GRID_WIDTH = 80
ROWS = 16

X, Y, ZH, ZL, C = 4, 4, 2, 4, 2
J = 3

MARK = 16384.0
MARK_SUM = 1.0e5
LOW = -1.0e30

K, KT, Q, QT, V, VT = range(6)
GROUPS = ((K, 1), (KT, 1), (Q, 2), (V, 1), (VT, 1))
RING = (K, KT, V, VT)


def device(x, y, z, c):
    return (y * (ZH * X) + lax.div(z, ZL) * X + x, lax.rem(z, ZL) * C + c)


def nt_dot(a, b):
    return lax.dot_general(a, b, (((1,), (1,)), ((), ())), preferred_element_type=jnp.float32)


def nn_dot(a, b):
    return jnp.dot(a, b, preferred_element_type=jnp.float32)


def kernel(
    q_in, k_in, v_in, qt_in, kt_in, vt_in, frame_ref, count_ref,
    o_out, ot_out,
    raw, send, kv, s_ref, p_ref, w_ref, acc_p, acc_w, acc_t, mx, lsum, gsum, outsend, outland, final,
    isem, dsem, rsem, ssem, dsend, rsend, bsend, osem, osend, fsem,
):
    Z = ZH * ZL
    heads = Z * J
    span = Z * ROWS
    chunks = X * C
    half = Y // 2
    keys = Y * span
    scale = 1.0 / math.sqrt(HD)
    scale2 = scale * math.log2(math.e)

    blk = lax.axis_index("blk")
    hd = lax.axis_index("head")
    x = lax.rem(blk, X)
    y = lax.div(blk, ZH * X)
    z = lax.rem(lax.div(blk, X), ZH) * ZL + lax.div(hd, C)
    c = lax.rem(hd, C)
    right = device(lax.rem(x + 1, X), y, z, c)
    left = device(lax.rem(x + X - 1, X), y, z, c)
    sib = device(x, y, z, 1 - c)
    own = (x * C + c) * Y
    computes = y < J

    def fetch(ref, slot):
        return pltpu.make_async_copy(ref, raw.at[slot], isem.at[slot])

    inputs = ((k_in, K), (kt_in, KT), (q_in, Q), (qt_in, QT), (v_in, V), (vt_in, VT))
    for ref, slot in inputs:
        fetch(ref, slot).start()

    barrier = pltpu.get_barrier_semaphore()

    def around(i):
        m = lax.div(i + 1, 2)
        return lax.rem(z + jnp.where(lax.rem(i, 2) == 1, m, Z - m), Z)

    def greet(i, carry):
        gz = around(Z - 1 - i)
        for gy in range(Y):

            @pl.when(jnp.logical_or(gy != y, gz != z))
            def _():
                pl.semaphore_signal(barrier, inc=1, device_id=device(x, gy, gz, c))

        return carry

    lax.fori_loop(0, Z, greet, 0)
    for other in (right, left, sib):
        pl.semaphore_signal(barrier, inc=1, device_id=other)

    row = lax.broadcasted_iota(jnp.int32, (ROWS, HD), 0)
    lane = lax.broadcasted_iota(jnp.int32, (ROWS, HD), 1)
    frame = jnp.zeros((ROWS, HD), jnp.float32)
    for i in range(ROWS):
        frame = jnp.where(row == i, frame_ref[hd * ROWS + i].astype(jnp.float32), frame)
    valid = hd * ROWS + row < count_ref[0]
    token = blk * (ROWS * ZL * C) + hd * ROWS + row
    token = jnp.where(token >= FRAME_TOKENS, token - FRAME_TOKENS, token).astype(jnp.float32)
    height = jnp.floor((token + 0.5) * (1.0 / GRID_WIDTH))
    across = token - height * GRID_WIDTH
    pair = lax.rem(lane, HD // 2)
    spatial = HD // 6
    temporal = HD // 2 - 2 * spatial
    is_frame = pair < temporal
    is_height = pair < temporal + spatial
    index = jnp.where(is_frame, pair, jnp.where(is_height, pair - temporal, pair - temporal - spatial))
    count = jnp.where(is_frame, float(temporal), float(spatial))
    freqs = jnp.exp(-math.log(10000.0) * index.astype(jnp.float32) / count)
    angles = jnp.where(is_frame, frame, jnp.where(is_height, height, across)) * freqs
    cosine = jnp.cos(angles)
    sine = jnp.sin(angles)
    sine = jnp.where(lane < HD // 2, -sine, sine)

    def rotate(ref, slot, marked=False):
        fetch(ref, slot).wait()
        for h in range(heads):
            wide = raw[slot, :, h * HD : (h + 1) * HD].astype(jnp.float32)
            turned = wide * cosine + pltpu.roll(wide, HD // 2, 1) * sine
            if marked:
                turned = jnp.where(valid, turned, MARK)
            send[h, slot] = turned.astype(jnp.bfloat16)

    def place(ref, slot):
        fetch(ref, slot).wait()
        for h in range(heads):
            send[h, slot] = raw[slot, :, h * HD : (h + 1) * HD]

    def direct(g):
        first, count = GROUPS[g]

        def step(i, carry):
            tz = around(i)
            for j in range(J):
                src = send.at[tz * J + j, pl.ds(first, count)]
                dst = kv.at[pl.ds(first, count), own + y, pl.ds(z * ROWS, ROWS)]
                here = jnp.logical_and(tz == z, y == j)

                @pl.when(here)
                def _():
                    pltpu.make_async_copy(src, dst, dsem.at[g]).start()

                @pl.when(jnp.logical_not(here))
                def _():
                    pltpu.make_async_remote_copy(
                        src_ref=src, dst_ref=dst, send_sem=dsend.at[g], recv_sem=dsem.at[g],
                        device_id=device(x, j, tz, c),
                    ).start()

            return carry

        lax.fori_loop(0, Z, step, 0)

    def sent(g, count):
        first, arrays = GROUPS[g]
        part = send.at[pl.ds(0, count), pl.ds(first, arrays)]
        pltpu.make_async_copy(part, part, dsend.at[g]).wait()

    def wait_direct(g):
        first, count = GROUPS[g]
        region = kv.at[pl.ds(first, count), pl.ds(own, Y)]
        pltpu.make_async_copy(region, region, dsem.at[g]).wait()

    def region(a, sx, sc, u):
        return kv.at[a, pl.ds((sx * C + sc) * Y + u * half, half)]

    def ring_send(a, part, to, event):
        n = RING.index(a)
        pltpu.make_async_remote_copy(
            src_ref=part, dst_ref=part, send_sem=rsend.at[n], recv_sem=rsem.at[n, event],
            device_id=to,
        ).start()

    def sib_send(a, part, event):
        n = RING.index(a)
        pltpu.make_async_remote_copy(
            src_ref=part, dst_ref=part, send_sem=bsend.at[n], recv_sem=ssem.at[n, event],
            device_id=sib,
        ).start()

    def start_own(a):
        first, second = region(a, x, c, 0), region(a, x, c, 1)
        ring_send(a, first, right, 2)
        ring_send(a, second, left, 3)
        ring_send(a, second, right, 4)
        ring_send(a, first, left, 5)
        sib_send(a, first, 0)
        sib_send(a, second, 1)

    def origin(i):
        far = jnp.where(i >= 6, 2, jnp.where(i >= 2, 1, 0))
        even = lax.rem(i, 2) == 0
        sx = lax.rem(jnp.where(even, x + X - far, x + far), X)
        swap = jnp.logical_or(i == 4, i == 5)
        u = jnp.where(jnp.logical_xor(even, swap), 0, 1)
        return sx, u

    def event(a, i):
        n = RING.index(a)
        sx, u = origin(i)
        part = region(a, sx, c, u)
        pltpu.make_async_copy(part, part, rsem.at[n, i]).wait()

        @pl.when(i == 2)
        def _():
            ring_send(a, part, right, 6)

        @pl.when(i == 3)
        def _():
            ring_send(a, part, left, 7)

        sib_send(a, part, i)

    def events(a, start, stop):
        def step(i, carry):
            event(a, i)
            return carry

        lax.fori_loop(start, stop, step, 0)

    def wait_sib(a, i):
        sx, u = origin(i)
        part = region(a, sx, 1 - c, u)
        pltpu.make_async_copy(part, part, ssem.at[RING.index(a), i]).wait()

    def wait_sibs(a):
        def step(i, carry):
            wait_sib(a, i)
            return carry

        lax.fori_loop(0, 8, step, 0)

    def queries_of(a):
        return kv[a, pl.ds(own, Y)].reshape(keys, HD)

    def chunk(a, i):
        return kv[a, pl.ds(i * Y, Y)].reshape(keys, HD)

    def unit(a, i):
        return kv[a, pl.ds(i * half, half)].reshape(keys // 2, HD)

    def lanes(op, total, array):
        for t in range(array.shape[1] // HD):
            total = op(total, array[:, t * HD : (t + 1) * HD])
        return total

    def scores(i):
        s = nt_dot(queries_of(Q), chunk(K, i))
        tail = keys - span
        marks = nt_dot(jnp.ones((8, HD), jnp.bfloat16), kv[K, i * Y + Y - 1])[0:1]
        last = jnp.where(marks > MARK_SUM, LOW, s[:, tail:])
        s = jnp.concatenate([s[:, :tail], last], axis=1)
        s_ref[i] = s
        mx[...] = lanes(jnp.maximum, mx[...], s)

    def weights(i):
        top = jnp.concatenate([mx[...]] * (keys // HD), axis=1)
        p = jnp.exp2(s_ref[i] * scale2 - top)
        g = nt_dot(
            jnp.concatenate([queries_of(QT), queries_of(Q)], axis=1),
            jnp.concatenate([chunk(K, i), chunk(KT, i)], axis=1),
        )
        w = p * g
        lsum[...] = lanes(jnp.add, lsum[...], p)
        gsum[...] = lanes(jnp.add, gsum[...], w)
        p = p.astype(jnp.bfloat16)
        w = w.astype(jnp.bfloat16)
        for u in range(2):
            p_ref[2 * i + u] = p[:, u * (keys // 2) : (u + 1) * (keys // 2)]
            w_ref[2 * i + u] = w[:, u * (keys // 2) : (u + 1) * (keys // 2)]

    def value_products(i):
        p = jnp.concatenate([p_ref[2 * i], p_ref[2 * i + 1]], axis=1)
        w = jnp.concatenate([w_ref[2 * i], w_ref[2 * i + 1]], axis=1)
        v = chunk(V, i)
        acc_p[...] += nn_dot(p, v)
        acc_w[...] += nn_dot(w, v)

    def give(which, ty):
        def step(i, carry):
            tz = around(i)
            src = outsend.at[which, ty * Z + tz]
            dst = outland.at[which, z * J + y]
            here = jnp.logical_and(tz == z, y == ty)

            @pl.when(here)
            def _():
                pltpu.make_async_copy(src, dst, osem.at[which]).start()

            @pl.when(jnp.logical_not(here))
            def _():
                pltpu.make_async_remote_copy(
                    src_ref=src, dst_ref=dst, send_sem=osend.at[which], recv_sem=osem.at[which],
                    device_id=device(x, ty, tz, c),
                ).start()

            return carry

        lax.fori_loop(0, Z, step, 0)

    rotate(k_in, K, True)
    pl.semaphore_wait(barrier, Y * Z - 1 + 3)
    direct(0)
    rotate(kt_in, KT)

    @pl.when(computes)
    def _():
        remote = heads - 1

        def begin(g, a):
            wait_direct(g)
            start_own(a)
            sent(g, remote)

        def loop(work):
            def step(i, carry):
                work(i)
                return carry

            lax.fori_loop(0, chunks, step, 0)

        begin(0, K)
        direct(1)
        rotate(q_in, Q)
        rotate(qt_in, QT)
        events(K, 2, 4)
        place(v_in, V)
        place(vt_in, VT)
        events(K, 4, 6)
        begin(1, KT)
        direct(2)
        mx[...] = jnp.full_like(mx, LOW)
        lsum[...] = jnp.zeros_like(lsum)
        gsum[...] = jnp.zeros_like(gsum)
        acc_p[...] = jnp.zeros_like(acc_p)
        acc_w[...] = jnp.zeros_like(acc_w)
        acc_t[...] = jnp.zeros_like(acc_t)
        events(K, 6, 8)
        events(KT, 2, 6)
        wait_direct(2)
        sent(2, remote)
        direct(3)
        wait_sibs(K)

        def first(i):
            @pl.when(jnp.logical_or(i == 2, i == 3))
            def _():
                event(KT, i + 4)

            @pl.when(i == 6)
            def _():
                begin(3, V)
                direct(4)

            scores(i)

        loop(first)
        mx[...] = jnp.broadcast_to(jnp.max(mx[...], axis=1, keepdims=True) * scale2, mx.shape)
        wait_sibs(KT)

        def second(i):
            @pl.when(i < 6)
            def _():
                event(V, i + 2)

            @pl.when(i == 6)
            def _():
                begin(4, VT)

            weights(i)

        loop(second)
        wait_sibs(V)

        def third(i):
            @pl.when(jnp.logical_or(i == 2, i == 3))
            def _():
                event(VT, i)

            value_products(i)

        loop(third)
        inverse = 1.0 / jnp.sum(lsum[...], axis=1, keepdims=True)
        slope = jnp.sum(gsum[...], axis=1, keepdims=True) * inverse * scale
        attended = acc_p[...] * inverse
        outsend[0] = attended.astype(jnp.bfloat16).reshape(Y * Z, ROWS, HD)
        for ty in range(Y):
            give(0, ty)
        lsum[...] = jnp.broadcast_to(inverse, lsum.shape)
        acc_w[...] = acc_w[...] * (inverse * scale) - slope * attended

        def fourth(i):
            @pl.when(i >= 4)
            def _():
                event(VT, i)

            wait_sib(VT, i)
            sx, u = origin(i)
            mine = (sx * C + c) * 2 + u
            other = (sx * C + 1 - c) * 2 + u
            acc_t[...] += nn_dot(
                jnp.concatenate([p_ref[mine], p_ref[other]], axis=1),
                jnp.concatenate([unit(VT, mine), unit(VT, other)], axis=0),
            )

        loop(fourth)
        for ty in range(Y):
            rows = slice(ty * span, (ty + 1) * span)
            tangent = acc_t[rows] * lsum[rows] + acc_w[rows]
            outsend[1, ty * Z : (ty + 1) * Z] = tangent.astype(jnp.bfloat16).reshape(Z, ROWS, HD)
            give(1, ty)

    @pl.when(jnp.logical_not(computes))
    def _():
        sent(0, heads)
        direct(1)
        rotate(q_in, Q)
        rotate(qt_in, QT)
        sent(1, heads)
        direct(2)
        place(v_in, V)
        place(vt_in, VT)
        sent(2, heads)
        direct(3)
        sent(3, heads)
        direct(4)
        sent(4, heads)

    def finish(which, out):
        pltpu.make_async_copy(outland.at[which], outland.at[which], osem.at[which]).wait()
        for h in range(heads):
            final[which, :, h * HD : (h + 1) * HD] = outland[which, h]
        pltpu.make_async_copy(final.at[which], out, fsem.at[which]).start()

    finish(0, o_out)
    finish(1, ot_out)
    pltpu.make_async_copy(final.at[0], o_out, fsem.at[0]).wait()
    pltpu.make_async_copy(final.at[1], ot_out, fsem.at[1]).wait()

    @pl.when(computes)
    def _():
        for n in range(4):
            part = kv.at[0, pl.ds(0, 6 * half)]
            pltpu.make_async_copy(part, part, rsend.at[n]).wait()
            part = kv.at[0, pl.ds(0, 8 * half)]
            pltpu.make_async_copy(part, part, bsend.at[n]).wait()
        for which in range(2):
            part = outsend.at[which, pl.ds(0, Y * Z - 1)]
            pltpu.make_async_copy(part, part, osend.at[which]).wait()


def shards(queries, key_vectors, values, query_tangent, key_tangent, value_tangent,
           frame_index, valid_counts):
    Z = ZH * ZL
    heads = Z * J
    span = Z * ROWS
    rows = Y * span
    chunks = X * C
    hbm = pl.BlockSpec(memory_space=pl.ANY)
    smem = pl.BlockSpec(memory_space=pltpu.SMEM)
    out = jax.ShapeDtypeStruct((ROWS, heads * HD), jnp.bfloat16)
    return pl.pallas_call(
        kernel,
        out_shape=(out, out),
        in_specs=[hbm] * 6 + [smem] * 2,
        out_specs=(hbm, hbm),
        scratch_shapes=[
            pltpu.VMEM((6, ROWS, heads * HD), jnp.bfloat16),
            pltpu.VMEM((heads, 6, ROWS, HD), jnp.bfloat16),
            pltpu.VMEM((6, chunks * Y, span, HD), jnp.bfloat16),
            pltpu.VMEM((chunks, rows, rows), jnp.float32),
            pltpu.VMEM((2 * chunks, rows, rows // 2), jnp.bfloat16),
            pltpu.VMEM((2 * chunks, rows, rows // 2), jnp.bfloat16),
            pltpu.VMEM((rows, HD), jnp.float32),
            pltpu.VMEM((rows, HD), jnp.float32),
            pltpu.VMEM((rows, HD), jnp.float32),
            pltpu.VMEM((rows, HD), jnp.float32),
            pltpu.VMEM((rows, HD), jnp.float32),
            pltpu.VMEM((rows, HD), jnp.float32),
            pltpu.VMEM((2, Y * Z, ROWS, HD), jnp.bfloat16),
            pltpu.VMEM((2, heads, ROWS, HD), jnp.bfloat16),
            pltpu.VMEM((2, ROWS, heads * HD), jnp.bfloat16),
            pltpu.SemaphoreType.DMA((6,)),
            pltpu.SemaphoreType.DMA((5,)),
            pltpu.SemaphoreType.DMA((4, 8)),
            pltpu.SemaphoreType.DMA((4, 8)),
            pltpu.SemaphoreType.DMA((5,)),
            pltpu.SemaphoreType.DMA((4,)),
            pltpu.SemaphoreType.DMA((4,)),
            pltpu.SemaphoreType.DMA((2,)),
            pltpu.SemaphoreType.DMA((2,)),
            pltpu.SemaphoreType.DMA((2,)),
        ],
        compiler_params=pltpu.CompilerParams(
            collective_id=0, has_side_effects=True, vmem_limit_bytes=52 * 1024 * 1024
        ),
    )(queries, key_vectors, values, query_tangent, key_tangent, value_tangent,
      frame_index, valid_counts)


def solution(mesh):
    tokens = P(("blk", "head"), None)
    return jax.shard_map(
        shards,
        mesh=mesh,
        in_specs=(tokens,) * 6 + (P("blk"), P("blk")),
        out_specs=(tokens, tokens),
        check_vma=False,
    )
```

time: 68.3 us -> 77.2 us (1.13)
  Pallas kernels: 59.6 us -> 68.3 us
  other arithmetic: 1.21 us -> 0 us
  local copies, waits for them, and re-layouts: 5.82 us -> 6.63 us
    pallas_call x1, Pallas kernels: 59.6 us -> 68.3 us  [shards(): pl.pallas_call(kernel, out_shape=(out, out), in_specs=[hbm] * 6 + [smem]...]
    unnamed x14 -> x16, local copies, waits for them, and re-layouts: 5.75 us -> 6.63 us
where the time goes in v2:
time: 77.2 us; the launch traced here: 76.3 us
  Pallas kernels  68.3 us (88%)
  local copies, waits for them, and re-layouts  6.63 us (9%)
  between operations  1.33 us (2%)
    pallas_call x1, Pallas kernels, shards(): pl.pallas_call(kernel, out_shape=(out, out), in_specs=[hbm] * 6 + [smem]...  68.3 us
    unnamed x16, local copies, waits for them, and re-layouts  6.63 us

profile of v2, /device:TPU:1, one launch (start us, length us, event | category | flops | bytes accessed | tf_op | source)
XLA Modules:
  0.0 76.3 jit_solution(17145899592096160607)
XLA Ops:
  0.6 0.0 copy-start.6
  1.3 0.0 copy-done.6
  1.3 0.0 copy-start
  1.3 0.9 %copy-done = bf16[16,3072]{1,0:T(8,128)(2,1)S(1)} copy-done((bf16[16,3072]{1,0:T(8,128)(2,1)S(1)}, bf16[16,3072]{1,0:T(8,128)(2,1)}, u32[]{:S(2)}) %copy-start) | copy-done | bytes 98328
  2.2 0.0 copy-start.1
  2.2 0.9 %copy-done.1 = bf16[16,3072]{1,0:T(8,128)(2,1)S(1)} copy-done((bf16[16,3072]{1,0:T(8,128)(2,1)S(1)}, bf16[16,3072]{1,0:T(8,128)(2,1)}, u32[]{:S(2)}) %copy-start.1) | copy-done | bytes 98328
  3.1 0.0 copy-start.2
  3.1 0.9 %copy-done.2 = bf16[16,3072]{1,0:T(8,128)(2,1)S(1)} copy-done((bf16[16,3072]{1,0:T(8,128)(2,1)S(1)}, bf16[16,3072]{1,0:T(8,128)(2,1)}, u32[]{:S(2)}) %copy-start.2) | copy-done | bytes 98328
  4.0 0.0 copy-start.3
  4.0 0.9 %copy-done.3 = bf16[16,3072]{1,0:T(8,128)(2,1)S(1)} copy-done((bf16[16,3072]{1,0:T(8,128)(2,1)S(1)}, bf16[16,3072]{1,0:T(8,128)(2,1)}, u32[]{:S(2)}) %copy-start.3) | copy-done | bytes 98328
  4.9 0.0 copy-start.4
  4.9 0.9 %copy-done.4 = bf16[16,3072]{1,0:T(8,128)(2,1)S(1)} copy-done((bf16[16,3072]{1,0:T(8,128)(2,1)S(1)}, bf16[16,3072]{1,0:T(8,128)(2,1)}, u32[]{:S(2)}) %copy-start.4) | copy-done | bytes 98328
  5.8 0.0 copy-start.5
  5.8 0.9 %copy-done.5 = bf16[16,3072]{1,0:T(8,128)(2,1)S(1)} copy-done((bf16[16,3072]{1,0:T(8,128)(2,1)S(1)}, bf16[16,3072]{1,0:T(8,128)(2,1)}, u32[]{:S(2)}) %copy-start.5) | copy-done | bytes 98328
  6.7 68.3 %shard_map.95 = (bf16[16,3072]{1,0:T(8,128)(2,1)S(1)}, bf16[16,3072]{1,0:T(8,128)(2,1)S(1)}) custom-call(bf16[16,3072]{1,0:T(8,128)(2,1)S(1)} %copy-done, bf16[16,3072]{1,0:T(8,128)(2,1)S(1)} %copy-done.1, bf16[16,3072]{1,0:T(8,128)(2,1)S(1)} %copy-done.2, bf16[16,3072]{1,0:T(8,128)(2,1)S(1)} %copy-done.3, bf16[16,3072]{1,0:T(8,128)(2,1)S(1)} %copy-done.4, ...), custom_call_target="tpu_custom_call" | custom-call | tf_op jit(solution)/shard_map/pallas_call | solution.py:463
  75.0 0.6 copy.13
  75.7 0.6 copy.14
Async XLA Ops:
  0.6 0.7 copy-start.6
  1.3 0.9 %copy-start = (bf16[16,3072]{1,0:T(8,128)(2,1)S(1)}, bf16[16,3072]{1,0:T(8,128)(2,1)}, u32[]{:S(2)}) copy-start(bf16[16,3072]{1,0:T(8,128)(2,1)} %q_in.1) | copy-start | bytes 294916
  2.2 0.9 %copy-start.1 = (bf16[16,3072]{1,0:T(8,128)(2,1)S(1)}, bf16[16,3072]{1,0:T(8,128)(2,1)}, u32[]{:S(2)}) copy-start(bf16[16,3072]{1,0:T(8,128)(2,1)} %k_in.1) | copy-start | bytes 294916
  3.1 0.9 %copy-start.2 = (bf16[16,3072]{1,0:T(8,128)(2,1)S(1)}, bf16[16,3072]{1,0:T(8,128)(2,1)}, u32[]{:S(2)}) copy-start(bf16[16,3072]{1,0:T(8,128)(2,1)} %v_in.1) | copy-start | bytes 294916
  4.0 0.9 %copy-start.3 = (bf16[16,3072]{1,0:T(8,128)(2,1)S(1)}, bf16[16,3072]{1,0:T(8,128)(2,1)}, u32[]{:S(2)}) copy-start(bf16[16,3072]{1,0:T(8,128)(2,1)} %qt_in.1) | copy-start | bytes 294916
  4.9 0.9 %copy-start.4 = (bf16[16,3072]{1,0:T(8,128)(2,1)S(1)}, bf16[16,3072]{1,0:T(8,128)(2,1)}, u32[]{:S(2)}) copy-start(bf16[16,3072]{1,0:T(8,128)(2,1)} %kt_in.1) | copy-start | bytes 294916
  5.8 0.9 %copy-start.5 = (bf16[16,3072]{1,0:T(8,128)(2,1)S(1)}, bf16[16,3072]{1,0:T(8,128)(2,1)}, u32[]{:S(2)}) copy-start(bf16[16,3072]{1,0:T(8,128)(2,1)} %vt_in.1) | copy-start | bytes 294916

commit v3 on v2

v3 whole, which is shorter than its diff:
```python
import math

import jax
import jax.numpy as jnp
from jax import lax
from jax.experimental import pallas as pl
from jax.experimental.pallas import tpu as pltpu
from jax.sharding import PartitionSpec as P

HD = 128
FRAME_TOKENS = 3600
GRID_WIDTH = 80
ROWS = 16

X, Y, ZH, ZL, C = 4, 4, 2, 4, 2
J = 3

MARK = 16384.0
MARK_SUM = 1.0e5
LOW = -1.0e30

K, KT, Q, QT, V, VT = range(6)
GROUPS = ((K, 1), (KT, 1), (V, 1), (Q, 2), (VT, 1))
GROUP_OF = {K: 0, KT: 1, V: 2, Q: 3, VT: 4}
RING = (K, KT, V, VT)


def device(x, y, z, c):
    return (y * (ZH * X) + lax.div(z, ZL) * X + x, lax.rem(z, ZL) * C + c)


def nt_dot(a, b):
    return lax.dot_general(a, b, (((1,), (1,)), ((), ())), preferred_element_type=jnp.float32)


def nn_dot(a, b):
    return jnp.dot(a, b, preferred_element_type=jnp.float32)


def kernel(
    q_in, k_in, v_in, qt_in, kt_in, vt_in, frame_ref, count_ref,
    o_out, ot_out,
    raw, send, kv, s_ref, p_ref, w_ref, acc_p, acc_w, acc_t, mx, lsum, gsum, outsend, outland, final,
    isem, dsem, rsem, ssem, dsend, rsend, bsend, osem, osend, fsem,
):
    Z = ZH * ZL
    heads = Z * J
    span = Z * ROWS
    chunks = X * C
    near = Z // 2
    rows = Y * span
    side = rows // 2
    scale = 1.0 / math.sqrt(HD)
    scale2 = scale * math.log2(math.e)

    blk = lax.axis_index("blk")
    hd = lax.axis_index("head")
    x = lax.rem(blk, X)
    y = lax.div(blk, ZH * X)
    z = lax.rem(lax.div(blk, X), ZH) * ZL + lax.div(hd, C)
    c = lax.rem(hd, C)
    right = device(lax.rem(x + 1, X), y, z, c)
    left = device(lax.rem(x + X - 1, X), y, z, c)
    sib = device(x, y, z, 1 - c)
    own = (x * C + c) * 2
    computes = y < J

    def fetch(ref, slot):
        return pltpu.make_async_copy(ref, raw.at[slot], isem.at[slot])

    inputs = ((k_in, K), (kt_in, KT), (v_in, V), (q_in, Q), (qt_in, QT), (vt_in, VT))
    for ref, slot in inputs:
        fetch(ref, slot).start()

    barrier = pltpu.get_barrier_semaphore()

    def greet(i, carry):
        gz = lax.rem(z + near + i, Z)
        for gy in range(Y):

            @pl.when(jnp.logical_or(gy != y, gz != z))
            def _():
                pl.semaphore_signal(barrier, inc=1, device_id=device(x, gy, gz, c))

        return carry

    lax.fori_loop(0, Z, greet, 0)
    for other in (right, left, sib):
        pl.semaphore_signal(barrier, inc=1, device_id=other)

    row = lax.broadcasted_iota(jnp.int32, (ROWS, HD), 0)
    lane = lax.broadcasted_iota(jnp.int32, (ROWS, HD), 1)
    frame = jnp.zeros((ROWS, HD), jnp.float32)
    for i in range(ROWS):
        frame = jnp.where(row == i, frame_ref[hd * ROWS + i].astype(jnp.float32), frame)
    valid = hd * ROWS + row < count_ref[0]
    token = blk * (ROWS * ZL * C) + hd * ROWS + row
    token = jnp.where(token >= FRAME_TOKENS, token - FRAME_TOKENS, token).astype(jnp.float32)
    height = jnp.floor((token + 0.5) * (1.0 / GRID_WIDTH))
    across = token - height * GRID_WIDTH
    pair = lax.rem(lane, HD // 2)
    spatial = HD // 6
    temporal = HD // 2 - 2 * spatial
    is_frame = pair < temporal
    is_height = pair < temporal + spatial
    index = jnp.where(is_frame, pair, jnp.where(is_height, pair - temporal, pair - temporal - spatial))
    count = jnp.where(is_frame, float(temporal), float(spatial))
    freqs = jnp.exp(-math.log(10000.0) * index.astype(jnp.float32) / count)
    angles = jnp.where(is_frame, frame, jnp.where(is_height, height, across)) * freqs
    cosine = jnp.cos(angles)
    sine = jnp.sin(angles)
    sine = jnp.where(lane < HD // 2, -sine, sine)

    def rotate(ref, slot, marked=False):
        fetch(ref, slot).wait()
        for h in range(heads):
            wide = raw[slot, :, h * HD : (h + 1) * HD].astype(jnp.float32)
            turned = wide * cosine + pltpu.roll(wide, HD // 2, 1) * sine
            if marked:
                turned = jnp.where(valid, turned, MARK)
            send[h, slot] = turned.astype(jnp.bfloat16)

    def place(ref, slot):
        fetch(ref, slot).wait()
        for h in range(heads):
            send[h, slot] = raw[slot, :, h * HD : (h + 1) * HD]

    def direct(a):
        g = GROUP_OF[a]
        first, count = GROUPS[g]

        def step(i, carry):
            tz = lax.rem(z + 2 + Z - i, Z)
            u = lax.div(i, near)
            slot = lax.rem(i, near)
            for j in range(J):
                src = send.at[tz * J + j, pl.ds(first, count)]
                dst = kv.at[pl.ds(first, count), own + u, y, pl.ds(slot * ROWS, ROWS)]
                here = jnp.logical_and(tz == z, y == j)

                @pl.when(here)
                def _():
                    pltpu.make_async_copy(src, dst, dsem.at[g, u]).start()

                @pl.when(jnp.logical_not(here))
                def _():
                    pltpu.make_async_remote_copy(
                        src_ref=src, dst_ref=dst, send_sem=dsend.at[g], recv_sem=dsem.at[g, u],
                        device_id=device(x, j, tz, c),
                    ).start()

            return carry

        lax.fori_loop(0, Z, step, 0)

    def wait_direct(a, u):
        g = GROUP_OF[a]
        first, count = GROUPS[g]
        region = kv.at[pl.ds(first, count), own + u]
        pltpu.make_async_copy(region, region, dsem.at[g, u]).wait()

    def ring_send(a, part, to, event):
        n = RING.index(a)
        pltpu.make_async_remote_copy(
            src_ref=part, dst_ref=part, send_sem=rsend.at[n], recv_sem=rsem.at[n, event],
            device_id=to,
        ).start()

    def sib_send(a, part, event):
        n = RING.index(a)
        pltpu.make_async_remote_copy(
            src_ref=part, dst_ref=part, send_sem=bsend.at[n], recv_sem=ssem.at[n, event],
            device_id=sib,
        ).start()

    def origin(i):
        far = jnp.where(i >= 6, 2, jnp.where(i >= 2, 1, 0))
        even = lax.rem(i, 2) == 0
        sx = lax.rem(jnp.where(even, x + X - far, x + far), X)
        swap = jnp.logical_or(i == 4, i == 5)
        u = jnp.where(jnp.logical_xor(even, swap), 0, 1)
        return sx, u

    def places(i):
        sx, u = origin(i)
        return (sx * C + c) * 2 + u, (sx * C + 1 - c) * 2 + u

    def start(a, u):
        wait_direct(a, u)
        part = kv.at[a, own + u]
        if u == 0:
            ring_send(a, part, right, 2)
            ring_send(a, part, left, 5)
        else:
            ring_send(a, part, left, 3)
            ring_send(a, part, right, 4)
        sib_send(a, part, u)

    def take(a, i):
        part = kv.at[a, places(jnp.int32(i))[0]]
        pltpu.make_async_copy(part, part, rsem.at[RING.index(a), i]).wait()
        if i == 2:
            ring_send(a, part, right, 6)
        if i == 3:
            ring_send(a, part, left, 7)
        sib_send(a, part, i)

    def wait_sib(a, i):
        part = kv.at[a, places(i)[1]]
        pltpu.make_async_copy(part, part, ssem.at[RING.index(a), i]).wait()

    def queries_of(a):
        return kv[a, pl.ds(own, 2)].reshape(rows, HD)

    def pair(a, i):
        mine, other = places(i)
        return jnp.concatenate(
            [kv[a, mine].reshape(side, HD), kv[a, other].reshape(side, HD)], axis=0
        )

    def lanes(op, total, array):
        for t in range(array.shape[1] // HD):
            total = op(total, array[:, t * HD : (t + 1) * HD])
        return total

    def scores(i):
        keys = pair(K, i)
        s = nt_dot(queries_of(Q), keys)
        parts = []
        for n in range(2):
            low, high = n * side, (n + 1) * side
            marks = nt_dot(jnp.ones((8, HD), jnp.bfloat16), keys[high - HD : high])[0:1]
            parts.append(s[:, low : high - HD])
            parts.append(jnp.where(marks > MARK_SUM, LOW, s[:, high - HD : high]))
        s = jnp.concatenate(parts, axis=1)
        s_ref[i] = s
        mx[...] = lanes(jnp.maximum, mx[...], s)

    def weights(i):
        top = jnp.concatenate([mx[...]] * (rows // HD), axis=1)
        p = jnp.exp2(s_ref[i] * scale2 - top)
        g = nt_dot(
            jnp.concatenate([queries_of(QT), queries_of(Q)], axis=1),
            jnp.concatenate([pair(K, i), pair(KT, i)], axis=1),
        )
        w = p * g
        lsum[...] = lanes(jnp.add, lsum[...], p)
        gsum[...] = lanes(jnp.add, gsum[...], w)
        p_ref[i] = p.astype(jnp.bfloat16)
        w_ref[i] = w.astype(jnp.bfloat16)

    def value_products(i):
        v = pair(V, i)
        acc_p[...] += nn_dot(p_ref[i], v)
        acc_w[...] += nn_dot(w_ref[i], v)

    def give(which, u):
        def step(k, carry):
            tz = lax.rem(z + u * near + k + Z - 2, Z)
            for ty in range(Y):
                src = outsend.at[which, (u * Y + ty) * near + k]
                dst = outland.at[which, z * J + y]
                here = jnp.logical_and(tz == z, y == ty)

                @pl.when(here)
                def _():
                    pltpu.make_async_copy(src, dst, osem.at[which]).start()

                @pl.when(jnp.logical_not(here))
                def _():
                    pltpu.make_async_remote_copy(
                        src_ref=src, dst_ref=dst, send_sem=osend.at[which],
                        recv_sem=osem.at[which], device_id=device(x, ty, tz, c),
                    ).start()

            return carry

        lax.fori_loop(0, near, step, 0)

    def loop(work, beside):
        def step(i, carry):
            for k, act in beside.items():
                pl.when(i == k)(act)
            work(i)
            return carry

        lax.fori_loop(0, chunks, step, 0)

    rotate(k_in, K, True)
    pl.semaphore_wait(barrier, Y * Z - 1 + 3)
    direct(K)
    rotate(kt_in, KT)
    direct(KT)
    place(v_in, V)
    direct(V)

    @pl.when(computes)
    def _():
        start(K, 0)
        rotate(q_in, Q)
        rotate(qt_in, QT)
        direct(Q)
        start(K, 1)
        place(vt_in, VT)
        direct(VT)
        start(KT, 0)
        mx[...] = jnp.full_like(mx, LOW)
        for ref in (lsum, gsum, acc_p, acc_w, acc_t):
            ref[...] = jnp.zeros_like(ref)
        take(K, 2)
        take(K, 3)
        start(KT, 1)
        take(K, 4)
        take(K, 5)
        start(V, 0)
        take(KT, 2)
        take(KT, 3)
        start(V, 1)
        take(K, 6)
        take(K, 7)
        take(KT, 4)
        take(KT, 5)
        wait_direct(Q, 0)
        wait_direct(Q, 1)

        def first(i):
            wait_sib(K, i)
            scores(i)

        loop(first, {
            1: lambda: start(VT, 0),
            2: lambda: take(V, 2),
            3: lambda: take(V, 3),
            4: lambda: start(VT, 1),
            5: lambda: take(KT, 6),
            6: lambda: take(KT, 7),
        })
        mx[...] = jnp.broadcast_to(jnp.max(mx[...], axis=1, keepdims=True) * scale2, mx.shape)

        def second(i):
            wait_sib(KT, i)
            weights(i)

        loop(second, {
            0: lambda: take(V, 4),
            1: lambda: take(V, 5),
            3: lambda: take(VT, 2),
            4: lambda: take(VT, 3),
            5: lambda: take(V, 6),
            6: lambda: take(V, 7),
        })

        def third(i):
            wait_sib(V, i)
            value_products(i)

        loop(third, {3: lambda: take(VT, 4), 4: lambda: take(VT, 5)})
        inverse = 1.0 / jnp.sum(lsum[...], axis=1, keepdims=True)
        slope = jnp.sum(gsum[...], axis=1, keepdims=True) * inverse * scale
        attended = acc_p[...] * inverse
        outsend[0] = attended.astype(jnp.bfloat16).reshape(Y * Z, ROWS, HD)
        give(0, 1)
        give(0, 0)
        lsum[...] = jnp.broadcast_to(inverse, lsum.shape)
        acc_w[...] = acc_w[...] * (inverse * scale) - slope * attended

        def fourth(i):
            wait_sib(VT, i)
            acc_t[...] += nn_dot(p_ref[i], pair(VT, i))

        loop(fourth, {6: lambda: take(VT, 6), 7: lambda: take(VT, 7)})
        for u in (1, 0):
            part = slice(u * side, (u + 1) * side)
            tangent = acc_t[part] * lsum[part] + acc_w[part]
            outsend[1, u * Y * near : (u + 1) * Y * near] = tangent.astype(
                jnp.bfloat16
            ).reshape(Y * near, ROWS, HD)
            give(1, u)

    @pl.when(jnp.logical_not(computes))
    def _():
        rotate(q_in, Q)
        rotate(qt_in, QT)
        direct(Q)
        place(vt_in, VT)
        direct(VT)

    def finish(which, out):
        pltpu.make_async_copy(outland.at[which], outland.at[which], osem.at[which]).wait()
        for h in range(heads):
            final[which, :, h * HD : (h + 1) * HD] = outland[which, h]
        pltpu.make_async_copy(final.at[which], out, fsem.at[which]).start()

    finish(0, o_out)
    finish(1, ot_out)

    def sent(count):
        for g, (first, arrays) in enumerate(GROUPS):
            part = send.at[pl.ds(0, count), pl.ds(first, arrays)]
            pltpu.make_async_copy(part, part, dsend.at[g]).wait()

    @pl.when(computes)
    def _():
        sent(heads - 1)
        for n in range(4):
            part = kv.at[0, pl.ds(0, 6)]
            pltpu.make_async_copy(part, part, rsend.at[n]).wait()
            part = kv.at[0, pl.ds(0, 8)]
            pltpu.make_async_copy(part, part, bsend.at[n]).wait()
        for which in range(2):
            part = outsend.at[which, pl.ds(0, Y * Z - 1)]
            pltpu.make_async_copy(part, part, osend.at[which]).wait()

    @pl.when(jnp.logical_not(computes))
    def _():
        sent(heads)

    pltpu.make_async_copy(final.at[0], o_out, fsem.at[0]).wait()
    pltpu.make_async_copy(final.at[1], ot_out, fsem.at[1]).wait()


def shards(queries, key_vectors, values, query_tangent, key_tangent, value_tangent,
           frame_index, valid_counts):
    Z = ZH * ZL
    heads = Z * J
    span = Z * ROWS
    rows = Y * span
    chunks = X * C
    hbm = pl.BlockSpec(memory_space=pl.ANY)
    smem = pl.BlockSpec(memory_space=pltpu.SMEM)
    out = jax.ShapeDtypeStruct((ROWS, heads * HD), jnp.bfloat16)
    return pl.pallas_call(
        kernel,
        out_shape=(out, out),
        in_specs=[hbm] * 6 + [smem] * 2,
        out_specs=(hbm, hbm),
        scratch_shapes=[
            pltpu.VMEM((6, ROWS, heads * HD), jnp.bfloat16),
            pltpu.VMEM((heads, 6, ROWS, HD), jnp.bfloat16),
            pltpu.VMEM((6, chunks * 2, Y, span // 2, HD), jnp.bfloat16),
            pltpu.VMEM((chunks, rows, rows), jnp.float32),
            pltpu.VMEM((chunks, rows, rows), jnp.bfloat16),
            pltpu.VMEM((chunks, rows, rows), jnp.bfloat16),
            pltpu.VMEM((rows, HD), jnp.float32),
            pltpu.VMEM((rows, HD), jnp.float32),
            pltpu.VMEM((rows, HD), jnp.float32),
            pltpu.VMEM((rows, HD), jnp.float32),
            pltpu.VMEM((rows, HD), jnp.float32),
            pltpu.VMEM((rows, HD), jnp.float32),
            pltpu.VMEM((2, Y * Z, ROWS, HD), jnp.bfloat16),
            pltpu.VMEM((2, heads, ROWS, HD), jnp.bfloat16),
            pltpu.VMEM((2, ROWS, heads * HD), jnp.bfloat16),
            pltpu.SemaphoreType.DMA((6,)),
            pltpu.SemaphoreType.DMA((5, 2)),
            pltpu.SemaphoreType.DMA((4, 8)),
            pltpu.SemaphoreType.DMA((4, 8)),
            pltpu.SemaphoreType.DMA((5,)),
            pltpu.SemaphoreType.DMA((4,)),
            pltpu.SemaphoreType.DMA((4,)),
            pltpu.SemaphoreType.DMA((2,)),
            pltpu.SemaphoreType.DMA((2,)),
            pltpu.SemaphoreType.DMA((2,)),
        ],
        compiler_params=pltpu.CompilerParams(
            collective_id=0, has_side_effects=True, vmem_limit_bytes=64 * 1024 * 1024
        ),
    )(queries, key_vectors, values, query_tangent, key_tangent, value_tangent,
      frame_index, valid_counts)


def solution(mesh):
    tokens = P(("blk", "head"), None)
    return jax.shard_map(
        shards,
        mesh=mesh,
        in_specs=(tokens,) * 6 + (P("blk"), P("blk")),
        out_specs=(tokens, tokens),
        check_vma=False,
    )
```

time: 77.2 us -> 60.1 us (0.78)
  the two profiles are of different devices: /device:TPU:1 before, /device:TPU:6 now
where the time goes in v3:
time: 60.1 us; the launch traced here: 60 us
  Pallas kernels  56.5 us (94%)
  local copies, waits for them, and re-layouts  2.22 us (4%)
  between operations  1.3 us (2%)
    pallas_call x1, Pallas kernels, shards(): pl.pallas_call(kernel, out_shape=(out, out), in_specs=[hbm] * 6 + [smem]...  56.5 us
    unnamed x4, local copies, waits for them, and re-layouts  2.22 us

profile of v3, /device:TPU:6, one launch (start us, length us, event | category | flops | bytes accessed | tf_op | source)
XLA Modules:
  0.0 60.0 jit_solution(12776218024326103467)
XLA Ops:
  1.3 56.5 %shard_map.95 = (bf16[16,3072]{1,0:T(8,128)(2,1)}, bf16[16,3072]{1,0:T(8,128)(2,1)}) custom-call(bf16[16,3072]{1,0:T(8,128)(2,1)} %q_in.1, bf16[16,3072]{1,0:T(8,128)(2,1)} %k_in.1, bf16[16,3072]{1,0:T(8,128)(2,1)} %v_in.1, bf16[16,3072]{1,0:T(8,128)(2,1)} %qt_in.1, bf16[16,3072]{1,0:T(8,128)(2,1)} %kt_in.1, bf16[16,3072]{1,0:T(8,128)(2,1)} %vt_in.1, ...), custom_call_target="tpu_custom_call" | custom-call | tf_op jit(solution)/shard_map/pallas_call | solution.py:432
  57.8 0.0 copy-start
  57.8 1.6 %copy.13 = bf16[16,3072]{1,0:T(8,128)(2,1)} copy(bf16[16,3072]{1,0:T(8,128)(2,1)} %get-tuple-element.4) | data formatting | bytes 196608
  59.3 0.0 copy-done
  59.3 0.6 %copy.14 = bf16[16,3072]{1,0:T(8,128)(2,1)} copy(bf16[16,3072]{1,0:T(8,128)(2,1)S(1)} %copy-done) | data formatting | bytes 196608
Async XLA Ops:
  57.8 1.6 %copy-start = (bf16[16,3072]{1,0:T(8,128)(2,1)S(1)}, bf16[16,3072]{1,0:T(8,128)(2,1)}, u32[]{:S(2)}) copy-start(bf16[16,3072]{1,0:T(8,128)(2,1)} %get-tuple-element.5) | copy-start | bytes 294916

commit v4 on v3

--- a/solution.py
+++ b/solution.py
@@ -16,7 +16,8 @@
 J = 3
 
 MARK = 16384.0
-MARK_SUM = 1.0e5
+MARK_FLOOR = 1000.0
+MARK_WEIGHT = -1048576.0
 LOW = -1.0e30
 
 K, KT, Q, QT, V, VT = range(6)
@@ -174,11 +175,9 @@
         ).start()
 
     def origin(i):
-        far = jnp.where(i >= 6, 2, jnp.where(i >= 2, 1, 0))
-        even = lax.rem(i, 2) == 0
-        sx = lax.rem(jnp.where(even, x + X - far, x + far), X)
-        swap = jnp.logical_or(i == 4, i == 5)
-        u = jnp.where(jnp.logical_xor(even, swap), 0, 1)
+        step = jnp.where(lax.rem(i, 2) == 0, X - 1, 1)
+        sx = lax.rem(x + jnp.where(i < 2, 0, jnp.where(i < 6, step, 2)), X)
+        u = jnp.where(i < 2, i, jnp.where(i < 6, lax.div(i - 2, 2), i - 6))
         return sx, u
 
     def places(i):
@@ -188,21 +187,26 @@
     def start(a, u):
         wait_direct(a, u)
         part = kv.at[a, own + u]
-        if u == 0:
-            ring_send(a, part, right, 2)
-            ring_send(a, part, left, 5)
+        ring_send(a, part, right, 2 + 2 * u)
+        ring_send(a, part, left, 3 + 2 * u)
+        sib_send(a, part, u)
+
+    def take(a, i):
+        n = RING.index(a)
+        place = places(jnp.int32(i))[0]
+        part = kv.at[a, place]
+        halves = kv.at[a, place, pl.ds(0, Y // 2)], kv.at[a, place, pl.ds(Y // 2, Y // 2)]
+        if i < 6:
+            pltpu.make_async_copy(part, part, rsem.at[n, i]).wait()
+            u = (i - 2) // 2
+            if i % 2 == 0:
+                ring_send(a, halves[0], right, 6 + 2 * u)
+            else:
+                ring_send(a, halves[1], left, 7 + 2 * u)
         else:
-            ring_send(a, part, left, 3)
-            ring_send(a, part, right, 4)
-        sib_send(a, part, u)
-
-    def take(a, i):
-        part = kv.at[a, places(jnp.int32(i))[0]]
-        pltpu.make_async_copy(part, part, rsem.at[RING.index(a), i]).wait()
-        if i == 2:
-            ring_send(a, part, right, 6)
-        if i == 3:
-            ring_send(a, part, left, 7)
+            u = i - 6
+            for side_of, half in enumerate(halves):
+                pltpu.make_async_copy(half, half, rsem.at[n, 6 + 2 * u + side_of]).wait()
         sib_send(a, part, i)
 
     def wait_sib(a, i):
@@ -212,47 +216,65 @@
     def queries_of(a):
         return kv[a, pl.ds(own, 2)].reshape(rows, HD)
 
-    def pair(a, i):
-        mine, other = places(i)
-        return jnp.concatenate(
-            [kv[a, mine].reshape(side, HD), kv[a, other].reshape(side, HD)], axis=0
-        )
+    def units(a, j):
+        parts = []
+        for n in range(2):
+            for place in places(2 * j + n):
+                parts.append(kv[a, place].reshape(side, HD))
+        return parts
+
+    def wait_sibs(a, j):
+        wait_sib(a, 2 * j)
+        wait_sib(a, 2 * j + 1)
 
     def lanes(op, total, array):
         for t in range(array.shape[1] // HD):
             total = op(total, array[:, t * HD : (t + 1) * HD])
         return total
 
-    def scores(i):
-        keys = pair(K, i)
-        s = nt_dot(queries_of(Q), keys)
-        parts = []
-        for n in range(2):
-            low, high = n * side, (n + 1) * side
-            marks = nt_dot(jnp.ones((8, HD), jnp.bfloat16), keys[high - HD : high])[0:1]
-            parts.append(s[:, low : high - HD])
-            parts.append(jnp.where(marks > MARK_SUM, LOW, s[:, high - HD : high]))
-        s = jnp.concatenate(parts, axis=1)
-        s_ref[i] = s
+    def scores(j):
+        wait_sibs(K, j)
+        keys = units(K, j)
+        last = side // Y
+        marks = []
+        for part in keys:
+            over = jnp.maximum(part[side - last :].astype(jnp.float32) - MARK_FLOOR, 0.0)
+            marks.append(jnp.zeros((side - last, HD), jnp.bfloat16))
+            marks.append(over.astype(jnp.bfloat16))
+        weight = jnp.full((rows, HD), MARK_WEIGHT, jnp.bfloat16)
+        s = nt_dot(
+            jnp.concatenate([queries_of(Q), weight], axis=1),
+            jnp.concatenate([jnp.concatenate(keys, axis=0), jnp.concatenate(marks, axis=0)], axis=1),
+        )
+        s_ref[j] = s
         mx[...] = lanes(jnp.maximum, mx[...], s)
 
-    def weights(i):
-        top = jnp.concatenate([mx[...]] * (rows // HD), axis=1)
-        p = jnp.exp2(s_ref[i] * scale2 - top)
+    def weights(j):
+        wait_sibs(KT, j)
+        top = jnp.concatenate([mx[...]] * (2 * rows // HD), axis=1)
+        p = jnp.exp2(s_ref[j] * scale2 - top)
         g = nt_dot(
             jnp.concatenate([queries_of(QT), queries_of(Q)], axis=1),
-            jnp.concatenate([pair(K, i), pair(KT, i)], axis=1),
+            jnp.concatenate(
+                [jnp.concatenate(units(K, j), axis=0), jnp.concatenate(units(KT, j), axis=0)], axis=1
+            ),
         )
         w = p * g
         lsum[...] = lanes(jnp.add, lsum[...], p)
         gsum[...] = lanes(jnp.add, gsum[...], w)
-        p_ref[i] = p.astype(jnp.bfloat16)
-        w_ref[i] = w.astype(jnp.bfloat16)
-
-    def value_products(i):
-        v = pair(V, i)
-        acc_p[...] += nn_dot(p_ref[i], v)
-        acc_w[...] += nn_dot(w_ref[i], v)
+        p_ref[j] = p.astype(jnp.bfloat16)
+        w_ref[j] = w.astype(jnp.bfloat16)
+
+    def stacked(a, steps):
+        parts = []
+        for j in steps:
+            wait_sibs(a, j)
+        for j in steps:
+            parts += units(a, j)
+        return jnp.concatenate(parts, axis=0)
+
+    def product(ref, steps, right_side):
+        return nn_dot(jnp.concatenate([ref[j] for j in steps], axis=1), right_side)
 
     def give(which, u):
         def step(k, carry):
@@ -277,14 +299,18 @@
 
         lax.fori_loop(0, near, step, 0)
 
-    def loop(work, beside):
+    def loop(work, low, high, beside=None):
         def step(i, carry):
-            for k, act in beside.items():
+            for k, act in (beside or {}).items():
                 pl.when(i == k)(act)
             work(i)
             return carry
 
-        lax.fori_loop(0, chunks, step, 0)
+        lax.fori_loop(low, high, step, 0)
+
+    def both(a, i):
+        take(a, i)
+        take(a, i + 1)
 
     rotate(k_in, K, True)
     pl.semaphore_wait(barrier, Y * Z - 1 + 3)
@@ -300,61 +326,49 @@
         rotate(q_in, Q)
         rotate(qt_in, QT)
         direct(Q)
-        start(K, 1)
         place(vt_in, VT)
         direct(VT)
+        start(K, 1)
         start(KT, 0)
+        start(KT, 1)
         mx[...] = jnp.full_like(mx, LOW)
-        for ref in (lsum, gsum, acc_p, acc_w, acc_t):
-            ref[...] = jnp.zeros_like(ref)
-        take(K, 2)
-        take(K, 3)
-        start(KT, 1)
-        take(K, 4)
-        take(K, 5)
+        lsum[...] = jnp.zeros_like(lsum)
+        gsum[...] = jnp.zeros_like(gsum)
+        both(K, 2)
         start(V, 0)
-        take(KT, 2)
-        take(KT, 3)
+        both(K, 4)
         start(V, 1)
+        both(KT, 2)
         take(K, 6)
-        take(K, 7)
-        take(KT, 4)
-        take(KT, 5)
+        both(KT, 4)
         wait_direct(Q, 0)
         wait_direct(Q, 1)
 
-        def first(i):
-            wait_sib(K, i)
-            scores(i)
-
-        loop(first, {
+        def before_last():
+            take(K, 7)
+            both(V, 2)
+
+        loop(scores, 0, 4, {
             1: lambda: start(VT, 0),
-            2: lambda: take(V, 2),
-            3: lambda: take(V, 3),
-            4: lambda: start(VT, 1),
-            5: lambda: take(KT, 6),
-            6: lambda: take(KT, 7),
+            2: lambda: start(VT, 1),
+            3: before_last,
         })
         mx[...] = jnp.broadcast_to(jnp.max(mx[...], axis=1, keepdims=True) * scale2, mx.shape)
-
-        def second(i):
-            wait_sib(KT, i)
-            weights(i)
-
-        loop(second, {
-            0: lambda: take(V, 4),
-            1: lambda: take(V, 5),
-            3: lambda: take(VT, 2),
-            4: lambda: take(VT, 3),
-            5: lambda: take(V, 6),
-            6: lambda: take(V, 7),
+        loop(weights, 0, 4, {
+            1: lambda: take(KT, 6),
+            2: lambda: both(V, 4),
+            3: lambda: take(KT, 7),
         })
-
-        def third(i):
-            wait_sib(V, i)
-            value_products(i)
-
-        loop(third, {3: lambda: take(VT, 4), 4: lambda: take(VT, 5)})
+        both(VT, 2)
+        early, late = range(3), range(3, 4)
+        v = stacked(V, early)
+        acc_p[...] = product(p_ref, early, v)
+        acc_w[...] = product(w_ref, early, v)
+        both(VT, 4)
+        both(V, 6)
+        v = stacked(V, late)
+        acc_p[...] += product(p_ref, late, v)
+        acc_w[...] += product(w_ref, late, v)
         inverse = 1.0 / jnp.sum(lsum[...], axis=1, keepdims=True)
         slope = jnp.sum(gsum[...], axis=1, keepdims=True) * inverse * scale
         attended = acc_p[...] * inverse
@@ -364,11 +378,9 @@
         lsum[...] = jnp.broadcast_to(inverse, lsum.shape)
         acc_w[...] = acc_w[...] * (inverse * scale) - slope * attended
 
-        def fourth(i):
-            wait_sib(VT, i)
-            acc_t[...] += nn_dot(p_ref[i], pair(VT, i))
-
-        loop(fourth, {6: lambda: take(VT, 6), 7: lambda: take(VT, 7)})
+        acc_t[...] = product(p_ref, early, stacked(VT, early))
+        both(VT, 6)
+        acc_t[...] += product(p_ref, late, stacked(VT, late))
         for u in (1, 0):
             part = slice(u * side, (u + 1) * side)
             tangent = acc_t[part] * lsum[part] + acc_w[part]
@@ -438,9 +450,9 @@
             pltpu.VMEM((6, ROWS, heads * HD), jnp.bfloat16),
             pltpu.VMEM((heads, 6, ROWS, HD), jnp.bfloat16),
             pltpu.VMEM((6, chunks * 2, Y, span // 2, HD), jnp.bfloat16),
-            pltpu.VMEM((chunks, rows, rows), jnp.float32),
-            pltpu.VMEM((chunks, rows, rows), jnp.bfloat16),
-            pltpu.VMEM((chunks, rows, rows), jnp.bfloat16),
+            pltpu.VMEM((chunks // 2, rows, 2 * rows), jnp.float32),
+            pltpu.VMEM((chunks // 2, rows, 2 * rows), jnp.bfloat16),
+            pltpu.VMEM((chunks // 2, rows, 2 * rows), jnp.bfloat16),
             pltpu.VMEM((rows, HD), jnp.float32),
             pltpu.VMEM((rows, HD), jnp.float32),
             pltpu.VMEM((rows, HD), jnp.float32),
@@ -452,7 +464,7 @@
             pltpu.VMEM((2, ROWS, heads * HD), jnp.bfloat16),
             pltpu.SemaphoreType.DMA((6,)),
             pltpu.SemaphoreType.DMA((5, 2)),
-            pltpu.SemaphoreType.DMA((4, 8)),
+            pltpu.SemaphoreType.DMA((4, 10)),
             pltpu.SemaphoreType.DMA((4, 8)),
             pltpu.SemaphoreType.DMA((5,)),
             pltpu.SemaphoreType.DMA((4,)),

time: 60.1 us -> 54.7 us (0.910)
  the two profiles are of different devices: /device:TPU:6 before, /device:TPU:1 now
where the time goes in v4:
time: 54.7 us; the launch traced here: 54.6 us
  Pallas kernels  51.1 us (93%)
  local copies, waits for them, and re-layouts  2.22 us (4%)
  between operations  1.3 us (2%)
    pallas_call x1, Pallas kernels, shards(): pl.pallas_call(kernel, out_shape=(out, out), in_specs=[hbm] * 6 + [smem]...  51.1 us
    unnamed x4, local copies, waits for them, and re-layouts  2.22 us

profile of v4, /device:TPU:1, one launch (start us, length us, event | category | flops | bytes accessed | tf_op | source)
XLA Modules:
  0.0 54.6 jit_solution(13961405294274162306)
XLA Ops:
  1.3 51.1 %shard_map.95 = (bf16[16,3072]{1,0:T(8,128)(2,1)}, bf16[16,3072]{1,0:T(8,128)(2,1)}) custom-call(bf16[16,3072]{1,0:T(8,128)(2,1)} %q_in.1, bf16[16,3072]{1,0:T(8,128)(2,1)} %k_in.1, bf16[16,3072]{1,0:T(8,128)(2,1)} %v_in.1, bf16[16,3072]{1,0:T(8,128)(2,1)} %qt_in.1, bf16[16,3072]{1,0:T(8,128)(2,1)} %kt_in.1, bf16[16,3072]{1,0:T(8,128)(2,1)} %vt_in.1, ...), custom_call_target="tpu_custom_call" | custom-call | tf_op jit(solution)/shard_map/pallas_call | solution.py:444
  52.3 0.0 copy-start
  52.4 1.6 %copy.13 = bf16[16,3072]{1,0:T(8,128)(2,1)} copy(bf16[16,3072]{1,0:T(8,128)(2,1)} %get-tuple-element.4) | data formatting | bytes 196608
  53.9 0.0 copy-done
  53.9 0.6 %copy.14 = bf16[16,3072]{1,0:T(8,128)(2,1)} copy(bf16[16,3072]{1,0:T(8,128)(2,1)S(1)} %copy-done) | data formatting | bytes 196608
Async XLA Ops:
  52.3 1.6 %copy-start = (bf16[16,3072]{1,0:T(8,128)(2,1)S(1)}, bf16[16,3072]{1,0:T(8,128)(2,1)}, u32[]{:S(2)}) copy-start(bf16[16,3072]{1,0:T(8,128)(2,1)} %get-tuple-element.5) | copy-start | bytes 294916

commit v5 on v4

--- a/solution.py
+++ b/solution.py
@@ -21,8 +21,8 @@
 LOW = -1.0e30
 
 K, KT, Q, QT, V, VT = range(6)
-GROUPS = ((K, 1), (KT, 1), (V, 1), (Q, 2), (VT, 1))
-GROUP_OF = {K: 0, KT: 1, V: 2, Q: 3, VT: 4}
+GROUPS = ((K, 1), (KT, 1), (Q, 2), (V, 1), (VT, 1))
+GROUP_OF = {K: 0, KT: 1, Q: 2, V: 3, VT: 4}
 RING = (K, KT, V, VT)
 
 
@@ -39,10 +39,11 @@
 
 
 def kernel(
-    q_in, k_in, v_in, qt_in, kt_in, vt_in, frame_ref, count_ref,
+    q_in, k_in, v_in, qt_in, kt_in, vt_in, frame_in, count_in,
     o_out, ot_out,
-    raw, send, kv, s_ref, p_ref, w_ref, acc_p, acc_w, acc_t, mx, lsum, gsum, outsend, outland, final,
-    isem, dsem, rsem, ssem, dsend, rsend, bsend, osem, osend, fsem,
+    frame_ref, count_ref, raw, send, kv, s_ref, p_ref, w_ref,
+    acc_p, acc_w, acc_t, mx, mx_late, alpha, lsum, gsum, outsend, outland, final,
+    small, isem, dsem, rsem, ssem, dsend, rsend, bsend, osem, osend, fsem,
 ):
     Z = ZH * ZL
     heads = Z * J
@@ -69,10 +70,6 @@
     def fetch(ref, slot):
         return pltpu.make_async_copy(ref, raw.at[slot], isem.at[slot])
 
-    inputs = ((k_in, K), (kt_in, KT), (v_in, V), (q_in, Q), (qt_in, QT), (vt_in, VT))
-    for ref, slot in inputs:
-        fetch(ref, slot).start()
-
     barrier = pltpu.get_barrier_semaphore()
 
     def greet(i, carry):
@@ -89,6 +86,16 @@
     for other in (right, left, sib):
         pl.semaphore_signal(barrier, inc=1, device_id=other)
 
+    inputs = ((k_in, K), (kt_in, KT), (q_in, Q), (qt_in, QT), (v_in, V), (vt_in, VT))
+    frames_copy = pltpu.make_async_copy(frame_in, frame_ref, small.at[0])
+    counts_copy = pltpu.make_async_copy(count_in, count_ref, small.at[1])
+    frames_copy.start()
+    counts_copy.start()
+    for ref, slot in inputs:
+        fetch(ref, slot).start()
+
+    frames_copy.wait()
+    counts_copy.wait()
     row = lax.broadcasted_iota(jnp.int32, (ROWS, HD), 0)
     lane = lax.broadcasted_iota(jnp.int32, (ROWS, HD), 1)
     frame = jnp.zeros((ROWS, HD), jnp.float32)
@@ -232,7 +239,7 @@
             total = op(total, array[:, t * HD : (t + 1) * HD])
         return total
 
-    def scores(j):
+    def scores(j, top):
         wait_sibs(K, j)
         keys = units(K, j)
         last = side // Y
@@ -247,11 +254,11 @@
             jnp.concatenate([jnp.concatenate(keys, axis=0), jnp.concatenate(marks, axis=0)], axis=1),
         )
         s_ref[j] = s
-        mx[...] = lanes(jnp.maximum, mx[...], s)
-
-    def weights(j):
+        top[...] = lanes(jnp.maximum, top[...], s)
+
+    def weights(j, top):
         wait_sibs(KT, j)
-        top = jnp.concatenate([mx[...]] * (2 * rows // HD), axis=1)
+        top = jnp.concatenate([top[...]] * (2 * rows // HD), axis=1)
         p = jnp.exp2(s_ref[j] * scale2 - top)
         g = nt_dot(
             jnp.concatenate([queries_of(QT), queries_of(Q)], axis=1),
@@ -273,8 +280,8 @@
             parts += units(a, j)
         return jnp.concatenate(parts, axis=0)
 
-    def product(ref, steps, right_side):
-        return nn_dot(jnp.concatenate([ref[j] for j in steps], axis=1), right_side)
+    def product(ref, steps, right_side, part=slice(None)):
+        return nn_dot(jnp.concatenate([ref[j, part] for j in steps], axis=1), right_side)
 
     def give(which, u):
         def step(k, carry):
@@ -317,85 +324,93 @@
     direct(K)
     rotate(kt_in, KT)
     direct(KT)
+    rotate(q_in, Q)
+    rotate(qt_in, QT)
+    direct(Q)
     place(v_in, V)
     direct(V)
+    place(vt_in, VT)
+    direct(VT)
 
     @pl.when(computes)
     def _():
         start(K, 0)
-        rotate(q_in, Q)
-        rotate(qt_in, QT)
-        direct(Q)
-        place(vt_in, VT)
-        direct(VT)
+        mx[...] = jnp.full_like(mx, LOW)
+        mx_late[...] = jnp.full_like(mx, LOW)
+        lsum[...] = jnp.zeros_like(lsum)
+        gsum[...] = jnp.zeros_like(gsum)
         start(K, 1)
         start(KT, 0)
         start(KT, 1)
-        mx[...] = jnp.full_like(mx, LOW)
-        lsum[...] = jnp.zeros_like(lsum)
-        gsum[...] = jnp.zeros_like(gsum)
         both(K, 2)
-        start(V, 0)
         both(K, 4)
-        start(V, 1)
-        both(KT, 2)
-        take(K, 6)
-        both(KT, 4)
         wait_direct(Q, 0)
         wait_direct(Q, 1)
-
-        def before_last():
-            take(K, 7)
+        loop(lambda j: scores(j, mx), 0, 3, {
+            1: lambda: both(KT, 2),
+            2: lambda: start(V, 0),
+        })
+        take(K, 6)
+        start(V, 1)
+        both(KT, 4)
+        mx[...] = jnp.broadcast_to(jnp.max(mx[...], axis=1, keepdims=True) * scale2, mx.shape)
+        take(K, 7)
+
+        def second():
+            start(VT, 0)
+            take(KT, 6)
+
+        def third():
+            start(VT, 1)
             both(V, 2)
 
-        loop(scores, 0, 4, {
-            1: lambda: start(VT, 0),
-            2: lambda: start(VT, 1),
-            3: before_last,
-        })
-        mx[...] = jnp.broadcast_to(jnp.max(mx[...], axis=1, keepdims=True) * scale2, mx.shape)
-        loop(weights, 0, 4, {
-            1: lambda: take(KT, 6),
-            2: lambda: both(V, 4),
-            3: lambda: take(KT, 7),
-        })
+        loop(lambda j: weights(j, mx), 0, 3, {1: second, 2: third})
+        scores(3, mx_late)
+        take(KT, 7)
+        both(V, 4)
+        top = jnp.maximum(mx[...], jnp.max(mx_late[...], axis=1, keepdims=True) * scale2)
+        factor = jnp.exp2(mx[...] - top)
+        alpha[...] = factor
+        mx[...] = top
+        lsum[...] = lsum[...] * factor
+        gsum[...] = gsum[...] * factor
+        weights(3, mx)
         both(VT, 2)
-        early, late = range(3), range(3, 4)
+        early, middle, late = range(2), range(2, 3), range(3, 4)
         v = stacked(V, early)
         acc_p[...] = product(p_ref, early, v)
         acc_w[...] = product(w_ref, early, v)
         both(VT, 4)
-        both(V, 6)
+        v = stacked(V, middle)
+        acc_p[...] += product(p_ref, middle, v)
+        acc_w[...] += product(w_ref, middle, v)
+        take(V, 6)
+        acc_t[...] = product(p_ref, early, stacked(VT, early))
+        take(V, 7)
         v = stacked(V, late)
-        acc_p[...] += product(p_ref, late, v)
-        acc_w[...] += product(w_ref, late, v)
         inverse = 1.0 / jnp.sum(lsum[...], axis=1, keepdims=True)
         slope = jnp.sum(gsum[...], axis=1, keepdims=True) * inverse * scale
-        attended = acc_p[...] * inverse
+        attended = (acc_p[...] * alpha[...] + product(p_ref, late, v)) * inverse
         outsend[0] = attended.astype(jnp.bfloat16).reshape(Y * Z, ROWS, HD)
         give(0, 1)
         give(0, 0)
+        acc_w[...] = (acc_w[...] * alpha[...] + product(w_ref, late, v)) * (
+            inverse * scale
+        ) - slope * attended
         lsum[...] = jnp.broadcast_to(inverse, lsum.shape)
-        acc_w[...] = acc_w[...] * (inverse * scale) - slope * attended
-
-        acc_t[...] = product(p_ref, early, stacked(VT, early))
-        both(VT, 6)
-        acc_t[...] += product(p_ref, late, stacked(VT, late))
+        take(VT, 6)
+        acc_t[...] = (acc_t[...] + product(p_ref, middle, stacked(VT, middle))) * (
+            alpha[...] * lsum[...]
+        ) + acc_w[...]
+        take(VT, 7)
+        v = stacked(VT, late)
         for u in (1, 0):
             part = slice(u * side, (u + 1) * side)
-            tangent = acc_t[part] * lsum[part] + acc_w[part]
+            tangent = acc_t[part] + product(p_ref, late, v, part) * lsum[part]
             outsend[1, u * Y * near : (u + 1) * Y * near] = tangent.astype(
                 jnp.bfloat16
             ).reshape(Y * near, ROWS, HD)
             give(1, u)
-
-    @pl.when(jnp.logical_not(computes))
-    def _():
-        rotate(q_in, Q)
-        rotate(qt_in, QT)
-        direct(Q)
-        place(vt_in, VT)
-        direct(VT)
 
     def finish(which, out):
         pltpu.make_async_copy(outland.at[which], outland.at[which], osem.at[which]).wait()
@@ -439,14 +454,15 @@
     rows = Y * span
     chunks = X * C
     hbm = pl.BlockSpec(memory_space=pl.ANY)
-    smem = pl.BlockSpec(memory_space=pltpu.SMEM)
     out = jax.ShapeDtypeStruct((ROWS, heads * HD), jnp.bfloat16)
     return pl.pallas_call(
         kernel,
         out_shape=(out, out),
-        in_specs=[hbm] * 6 + [smem] * 2,
+        in_specs=[hbm] * 8,
         out_specs=(hbm, hbm),
         scratch_shapes=[
+            pltpu.SMEM((ROWS * ZL * C,), jnp.int32),
+            pltpu.SMEM((1,), jnp.int32),
             pltpu.VMEM((6, ROWS, heads * HD), jnp.bfloat16),
             pltpu.VMEM((heads, 6, ROWS, HD), jnp.bfloat16),
             pltpu.VMEM((6, chunks * 2, Y, span // 2, HD), jnp.bfloat16),
@@ -459,9 +475,12 @@
             pltpu.VMEM((rows, HD), jnp.float32),
             pltpu.VMEM((rows, HD), jnp.float32),
             pltpu.VMEM((rows, HD), jnp.float32),
+            pltpu.VMEM((rows, HD), jnp.float32),
+            pltpu.VMEM((rows, HD), jnp.float32),
             pltpu.VMEM((2, Y * Z, ROWS, HD), jnp.bfloat16),
             pltpu.VMEM((2, heads, ROWS, HD), jnp.bfloat16),
             pltpu.VMEM((2, ROWS, heads * HD), jnp.bfloat16),
+            pltpu.SemaphoreType.DMA((2,)),
             pltpu.SemaphoreType.DMA((6,)),
             pltpu.SemaphoreType.DMA((5, 2)),
             pltpu.SemaphoreType.DMA((4, 10)),
@@ -474,7 +493,7 @@
             pltpu.SemaphoreType.DMA((2,)),
         ],
         compiler_params=pltpu.CompilerParams(
-            collective_id=0, has_side_effects=True, vmem_limit_bytes=64 * 1024 * 1024
+            collective_id=0, has_side_effects=True, vmem_limit_bytes=54975 * 1024
         ),
     )(queries, key_vectors, values, query_tangent, key_tangent, value_tangent,
       frame_index, valid_counts)

time: 54.7 us -> 54.1 us (0.989)
  local copies, waits for them, and re-layouts: 2.22 us -> 1.29 us
    unnamed x4, local copies, waits for them, and re-layouts: 2.22 us -> 1.29 us
where the time goes in v5:
time: 54.1 us; the launch traced here: 54 us
  Pallas kernels  51.4 us (95%)
  between operations  1.32 us (2%)
  local copies, waits for them, and re-layouts  1.29 us (2%)
    pallas_call x1, Pallas kernels, shards(): pl.pallas_call(kernel, out_shape=(out, out), in_specs=[hbm] * 8, out_spec...  51.4 us
    unnamed x4, local copies, waits for them, and re-layouts  1.29 us

profile of v5, /device:TPU:1, one launch (start us, length us, event | category | flops | bytes accessed | tf_op | source)
XLA Modules:
  0.0 54.0 jit_solution(7621735686630375529)
XLA Ops:
  0.6 0.0 copy-start
  1.3 0.0 copy-done
  1.3 51.4 %shard_map.95 = (bf16[16,3072]{1,0:T(8,128)(2,1)S(1)}, bf16[16,3072]{1,0:T(8,128)(2,1)S(1)}) custom-call(bf16[16,3072]{1,0:T(8,128)(2,1)} %q_in.1, bf16[16,3072]{1,0:T(8,128)(2,1)} %k_in.1, bf16[16,3072]{1,0:T(8,128)(2,1)} %v_in.1, bf16[16,3072]{1,0:T(8,128)(2,1)} %qt_in.1, bf16[16,3072]{1,0:T(8,128)(2,1)} %kt_in.1, bf16[16,3072]{1,0:T(8,128)(2,1)} %vt_in.1, ...), custom_call_target="tpu_custom_call" | custom-call | tf_op jit(solution)/shard_map/pallas_call | solution.py:458
  52.7 0.6 %copy.13 = bf16[16,3072]{1,0:T(8,128)(2,1)} copy(bf16[16,3072]{1,0:T(8,128)(2,1)S(1)} %get-tuple-element.4) | data formatting | bytes 196608
  53.3 0.6 %copy.14 = bf16[16,3072]{1,0:T(8,128)(2,1)} copy(bf16[16,3072]{1,0:T(8,128)(2,1)S(1)} %get-tuple-element.5) | data formatting | bytes 196608
Async XLA Ops:
  0.6 0.7 %copy-start = (s32[128]{0:T(128)S(1)}, s32[128]{0:T(128)}, u32[]{:S(2)}) copy-start(s32[128]{0:T(128)} %frame_in.1) | copy-start | bytes 1540

commit v6 on v5

--- a/solution.py
+++ b/solution.py
@@ -42,8 +42,8 @@
     q_in, k_in, v_in, qt_in, kt_in, vt_in, frame_in, count_in,
     o_out, ot_out,
     frame_ref, count_ref, raw, send, kv, s_ref, p_ref, w_ref,
-    acc_p, acc_w, acc_t, mx, mx_late, alpha, lsum, gsum, outsend, outland, final,
-    small, isem, dsem, rsem, ssem, dsend, rsend, bsend, osem, osend, fsem,
+    acc_p, acc_w, acc_t, mx, mx_late, alpha, lsum, gsum, outsend,
+    small, isem, dsem, rsem, ssem, dsend, rsend, bsend, osem, osend,
 ):
     Z = ZH * ZL
     heads = Z * J
@@ -70,28 +70,29 @@
     def fetch(ref, slot):
         return pltpu.make_async_copy(ref, raw.at[slot], isem.at[slot])
 
-    barrier = pltpu.get_barrier_semaphore()
-
-    def greet(i, carry):
-        gz = lax.rem(z + near + i, Z)
-        for gy in range(Y):
-
-            @pl.when(jnp.logical_or(gy != y, gz != z))
-            def _():
-                pl.semaphore_signal(barrier, inc=1, device_id=device(x, gy, gz, c))
-
-        return carry
-
-    lax.fori_loop(0, Z, greet, 0)
-    for other in (right, left, sib):
-        pl.semaphore_signal(barrier, inc=1, device_id=other)
-
-    inputs = ((k_in, K), (kt_in, KT), (q_in, Q), (qt_in, QT), (v_in, V), (vt_in, VT))
     frames_copy = pltpu.make_async_copy(frame_in, frame_ref, small.at[0])
     counts_copy = pltpu.make_async_copy(count_in, count_ref, small.at[1])
     frames_copy.start()
     counts_copy.start()
-    for ref, slot in inputs:
+    fetch(k_in, K).start()
+
+    barrier = pltpu.get_barrier_semaphore()
+
+    def greet(i, carry):
+        gz = lax.rem(z + near + i, Z)
+        for gy in range(Y):
+
+            @pl.when(jnp.logical_or(gy != y, gz != z))
+            def _():
+                pl.semaphore_signal(barrier, inc=1, device_id=device(x, gy, gz, c))
+
+        return carry
+
+    lax.fori_loop(0, Z, greet, 0)
+    for other in (right, left, sib):
+        pl.semaphore_signal(barrier, inc=1, device_id=other)
+
+    for ref, slot in ((kt_in, KT), (q_in, Q), (qt_in, QT), (v_in, V), (vt_in, VT)):
         fetch(ref, slot).start()
 
     frames_copy.wait()
@@ -284,11 +285,13 @@
         return nn_dot(jnp.concatenate([ref[j, part] for j in steps], axis=1), right_side)
 
     def give(which, u):
+        out = (o_out, ot_out)[which]
+
         def step(k, carry):
             tz = lax.rem(z + u * near + k + Z - 2, Z)
             for ty in range(Y):
                 src = outsend.at[which, (u * Y + ty) * near + k]
-                dst = outland.at[which, z * J + y]
+                dst = out.at[:, pl.ds(pl.multiple_of((z * J + y) * HD, HD), HD)]
                 here = jnp.logical_and(tz == z, y == ty)
 
                 @pl.when(here)
@@ -368,6 +371,11 @@
         scores(3, mx_late)
         take(KT, 7)
         both(V, 4)
+        early, middle, late = range(2), range(2, 3), range(3, 4)
+        v = stacked(V, early)
+        acc_p[...] = product(p_ref, early, v)
+        acc_w[...] = product(w_ref, early, v)
+        both(VT, 2)
         top = jnp.maximum(mx[...], jnp.max(mx_late[...], axis=1, keepdims=True) * scale2)
         factor = jnp.exp2(mx[...] - top)
         alpha[...] = factor
@@ -375,11 +383,6 @@
         lsum[...] = lsum[...] * factor
         gsum[...] = gsum[...] * factor
         weights(3, mx)
-        both(VT, 2)
-        early, middle, late = range(2), range(2, 3), range(3, 4)
-        v = stacked(V, early)
-        acc_p[...] = product(p_ref, early, v)
-        acc_w[...] = product(w_ref, early, v)
         both(VT, 4)
         v = stacked(V, middle)
         acc_p[...] += product(p_ref, middle, v)
@@ -387,22 +390,20 @@
         take(V, 6)
         acc_t[...] = product(p_ref, early, stacked(VT, early))
         take(V, 7)
+        acc_t[...] += product(p_ref, middle, stacked(VT, middle))
         v = stacked(V, late)
         inverse = 1.0 / jnp.sum(lsum[...], axis=1, keepdims=True)
         slope = jnp.sum(gsum[...], axis=1, keepdims=True) * inverse * scale
         attended = (acc_p[...] * alpha[...] + product(p_ref, late, v)) * inverse
         outsend[0] = attended.astype(jnp.bfloat16).reshape(Y * Z, ROWS, HD)
+        both(VT, 6)
         give(0, 1)
         give(0, 0)
         acc_w[...] = (acc_w[...] * alpha[...] + product(w_ref, late, v)) * (
             inverse * scale
         ) - slope * attended
         lsum[...] = jnp.broadcast_to(inverse, lsum.shape)
-        take(VT, 6)
-        acc_t[...] = (acc_t[...] + product(p_ref, middle, stacked(VT, middle))) * (
-            alpha[...] * lsum[...]
-        ) + acc_w[...]
-        take(VT, 7)
+        acc_t[...] = acc_t[...] * (alpha[...] * lsum[...]) + acc_w[...]
         v = stacked(VT, late)
         for u in (1, 0):
             part = slice(u * side, (u + 1) * side)
@@ -412,14 +413,8 @@
             ).reshape(Y * near, ROWS, HD)
             give(1, u)
 
-    def finish(which, out):
-        pltpu.make_async_copy(outland.at[which], outland.at[which], osem.at[which]).wait()
-        for h in range(heads):
-            final[which, :, h * HD : (h + 1) * HD] = outland[which, h]
-        pltpu.make_async_copy(final.at[which], out, fsem.at[which]).start()
-
-    finish(0, o_out)
-    finish(1, ot_out)
+    for which, out in ((0, o_out), (1, ot_out)):
+        pltpu.make_async_copy(out, out, osem.at[which]).wait()
 
     def sent(count):
         for g, (first, arrays) in enumerate(GROUPS):
@@ -441,9 +436,6 @@
     @pl.when(jnp.logical_not(computes))
     def _():
         sent(heads)
-
-    pltpu.make_async_copy(final.at[0], o_out, fsem.at[0]).wait()
-    pltpu.make_async_copy(final.at[1], ot_out, fsem.at[1]).wait()
 
 
 def shards(queries, key_vectors, values, query_tangent, key_tangent, value_tangent,
@@ -478,8 +470,6 @@
             pltpu.VMEM((rows, HD), jnp.float32),
             pltpu.VMEM((rows, HD), jnp.float32),
             pltpu.VMEM((2, Y * Z, ROWS, HD), jnp.bfloat16),
-            pltpu.VMEM((2, heads, ROWS, HD), jnp.bfloat16),
-            pltpu.VMEM((2, ROWS, heads * HD), jnp.bfloat16),
             pltpu.SemaphoreType.DMA((2,)),
             pltpu.SemaphoreType.DMA((6,)),
             pltpu.SemaphoreType.DMA((5, 2)),
@@ -490,7 +480,6 @@
             pltpu.SemaphoreType.DMA((4,)),
             pltpu.SemaphoreType.DMA((2,)),
             pltpu.SemaphoreType.DMA((2,)),
-            pltpu.SemaphoreType.DMA((2,)),
         ],
         compiler_params=pltpu.CompilerParams(
             collective_id=0, has_side_effects=True, vmem_limit_bytes=54975 * 1024

time: 54.1 us -> 52.3 us (0.967)
  Pallas kernels: 51.4 us -> 49.6 us
    pallas_call x1, Pallas kernels: 51.4 us -> 49.6 us  [shards(): pl.pallas_call(kernel, out_shape=(out, out), in_specs=[hbm] * 8, out_spec...]
where the time goes in v6:
time: 52.3 us; the launch traced here: 52.2 us
  Pallas kernels  49.6 us (95%)
  between operations  1.32 us (3%)
  local copies, waits for them, and re-layouts  1.29 us (2%)
    pallas_call x1, Pallas kernels, shards(): pl.pallas_call(kernel, out_shape=(out, out), in_specs=[hbm] * 8, out_spec...  49.6 us
    unnamed x4, local copies, waits for them, and re-layouts  1.29 us

profile of v6, /device:TPU:1, one launch (start us, length us, event | category | flops | bytes accessed | tf_op | source)
XLA Modules:
  0.0 52.2 jit_solution(2551693602135961050)
XLA Ops:
  0.6 0.0 copy-start
  1.3 0.0 copy-done
  1.3 49.6 %shard_map.95 = (bf16[16,3072]{1,0:T(8,128)(2,1)S(1)}, bf16[16,3072]{1,0:T(8,128)(2,1)S(1)}) custom-call(bf16[16,3072]{1,0:T(8,128)(2,1)} %q_in.1, bf16[16,3072]{1,0:T(8,128)(2,1)} %k_in.1, bf16[16,3072]{1,0:T(8,128)(2,1)} %v_in.1, bf16[16,3072]{1,0:T(8,128)(2,1)} %qt_in.1, bf16[16,3072]{1,0:T(8,128)(2,1)} %kt_in.1, bf16[16,3072]{1,0:T(8,128)(2,1)} %vt_in.1, ...), custom_call_target="tpu_custom_call" | custom-call | tf_op jit(solution)/shard_map/pallas_call | solution.py:450
  50.9 0.6 %copy.13 = bf16[16,3072]{1,0:T(8,128)(2,1)} copy(bf16[16,3072]{1,0:T(8,128)(2,1)S(1)} %get-tuple-element.4) | data formatting | bytes 196608
  51.5 0.6 %copy.14 = bf16[16,3072]{1,0:T(8,128)(2,1)} copy(bf16[16,3072]{1,0:T(8,128)(2,1)S(1)} %get-tuple-element.5) | data formatting | bytes 196608
Async XLA Ops:
  0.6 0.7 %copy-start = (s32[128]{0:T(128)S(1)}, s32[128]{0:T(128)}, u32[]{:S(2)}) copy-start(s32[128]{0:T(128)} %frame_in.1) | copy-start | bytes 1540

commit v7 on v6

--- a/solution.py
+++ b/solution.py
@@ -24,6 +24,7 @@
 GROUPS = ((K, 1), (KT, 1), (Q, 2), (V, 1), (VT, 1))
 GROUP_OF = {K: 0, KT: 1, Q: 2, V: 3, VT: 4}
 RING = (K, KT, V, VT)
+RELAYED = (KT,)
 
 
 def device(x, y, z, c):
@@ -42,8 +43,8 @@
     q_in, k_in, v_in, qt_in, kt_in, vt_in, frame_in, count_in,
     o_out, ot_out,
     frame_ref, count_ref, raw, send, kv, s_ref, p_ref, w_ref,
-    acc_p, acc_w, acc_t, mx, mx_late, alpha, lsum, gsum, outsend,
-    small, isem, dsem, rsem, ssem, dsend, rsend, bsend, osem, osend,
+    acc_p, acc_w, acc_t, mx, mx_late, alpha, lsum, gsum, outsend, passing,
+    small, isem, dsem, rsem, ssem, dsend, rsend, bsend, osem, osend, psem, psend,
 ):
     Z = ZH * ZL
     heads = Z * J
@@ -64,6 +65,8 @@
     right = device(lax.rem(x + 1, X), y, z, c)
     left = device(lax.rem(x + X - 1, X), y, z, c)
     sib = device(x, y, z, 1 - c)
+    across_x = lax.rem(x + 2, X)
+    relay = device(x, Y - 1, z, c)
     own = (x * C + c) * 2
     computes = y < J
 
@@ -91,6 +94,16 @@
     lax.fori_loop(0, Z, greet, 0)
     for other in (right, left, sib):
         pl.semaphore_signal(barrier, inc=1, device_id=other)
+
+    @pl.when(computes)
+    def _():
+        pl.semaphore_signal(barrier, inc=1, device_id=device(across_x, Y - 1, z, c))
+
+    @pl.when(jnp.logical_not(computes))
+    def _():
+        for j in range(J):
+            pl.semaphore_signal(barrier, inc=1, device_id=device(across_x, j, z, c))
+
 
     for ref, slot in ((kt_in, KT), (q_in, Q), (qt_in, QT), (v_in, V), (vt_in, VT)):
         fetch(ref, slot).start()
@@ -195,31 +208,41 @@
     def start(a, u):
         wait_direct(a, u)
         part = kv.at[a, own + u]
-        ring_send(a, part, right, 2 + 2 * u)
-        ring_send(a, part, left, 3 + 2 * u)
-        sib_send(a, part, u)
-
-    def take(a, i):
-        n = RING.index(a)
+        ring_send(a, part, right, u)
+        ring_send(a, part, left, u)
+        if a in RELAYED and u == 1:
+            r = RELAYED.index(a)
+            pltpu.make_async_remote_copy(
+                src_ref=part, dst_ref=passing.at[r, y], send_sem=rsend.at[RING.index(a)],
+                recv_sem=psem.at[r, y], device_id=relay,
+            ).start()
+        sib_send(a, part, 0)
+
+    def arrived(sem, units_of):
+        part = kv.at[0, pl.ds(0, units_of)]
+        pltpu.make_async_copy(part, part, sem).wait()
+
+    def unit_halves(a, i):
         place = places(jnp.int32(i))[0]
-        part = kv.at[a, place]
-        halves = kv.at[a, place, pl.ds(0, Y // 2)], kv.at[a, place, pl.ds(Y // 2, Y // 2)]
-        if i < 6:
-            pltpu.make_async_copy(part, part, rsem.at[n, i]).wait()
-            u = (i - 2) // 2
-            if i % 2 == 0:
-                ring_send(a, halves[0], right, 6 + 2 * u)
-            else:
-                ring_send(a, halves[1], left, 7 + 2 * u)
-        else:
-            u = i - 6
-            for side_of, half in enumerate(halves):
-                pltpu.make_async_copy(half, half, rsem.at[n, 6 + 2 * u + side_of]).wait()
-        sib_send(a, part, i)
-
-    def wait_sib(a, i):
-        part = kv.at[a, places(i)[1]]
-        pltpu.make_async_copy(part, part, ssem.at[RING.index(a), i]).wait()
+        half = Y // 2
+        return kv.at[a, place], kv.at[a, place, pl.ds(0, half)], kv.at[a, place, pl.ds(half, half)]
+
+    def neighbours(a, u):
+        arrived(rsem.at[RING.index(a), u], 2)
+        from_left, first, _ = unit_halves(a, 2 + 2 * u)
+        from_right, _, second = unit_halves(a, 3 + 2 * u)
+        if a not in RELAYED or u == 0:
+            ring_send(a, first, right, 2 + u)
+            ring_send(a, second, left, 2 + u)
+        sib_send(a, from_left, 1 + u)
+        sib_send(a, from_right, 1 + u)
+
+    def opposite(a, u):
+        arrived(rsem.at[RING.index(a), 2 + u], 1)
+        sib_send(a, unit_halves(a, 6 + u)[0], 3)
+
+    def wait_sibs(a, j):
+        arrived(ssem.at[RING.index(a), j], 2)
 
     def queries_of(a):
         return kv[a, pl.ds(own, 2)].reshape(rows, HD)
@@ -230,10 +253,6 @@
             for place in places(2 * j + n):
                 parts.append(kv[a, place].reshape(side, HD))
         return parts
-
-    def wait_sibs(a, j):
-        wait_sib(a, 2 * j)
-        wait_sib(a, 2 * j + 1)
 
     def lanes(op, total, array):
         for t in range(array.shape[1] // HD):
@@ -318,12 +337,8 @@
 
         lax.fori_loop(low, high, step, 0)
 
-    def both(a, i):
-        take(a, i)
-        take(a, i + 1)
-
     rotate(k_in, K, True)
-    pl.semaphore_wait(barrier, Y * Z - 1 + 3)
+    pl.semaphore_wait(barrier, Y * Z - 1 + 3 + jnp.where(computes, 1, J))
     direct(K)
     rotate(kt_in, KT)
     direct(KT)
@@ -345,37 +360,37 @@
         start(K, 1)
         start(KT, 0)
         start(KT, 1)
-        both(K, 2)
-        both(K, 4)
+        neighbours(K, 0)
+        neighbours(K, 1)
         wait_direct(Q, 0)
         wait_direct(Q, 1)
         loop(lambda j: scores(j, mx), 0, 3, {
-            1: lambda: both(KT, 2),
+            1: lambda: neighbours(KT, 0),
             2: lambda: start(V, 0),
         })
-        take(K, 6)
+        opposite(K, 0)
         start(V, 1)
-        both(KT, 4)
+        neighbours(KT, 1)
         mx[...] = jnp.broadcast_to(jnp.max(mx[...], axis=1, keepdims=True) * scale2, mx.shape)
-        take(K, 7)
+        opposite(K, 1)
 
         def second():
             start(VT, 0)
-            take(KT, 6)
+            opposite(KT, 0)
 
         def third():
             start(VT, 1)
-            both(V, 2)
+            neighbours(V, 0)
 
         loop(lambda j: weights(j, mx), 0, 3, {1: second, 2: third})
         scores(3, mx_late)
-        take(KT, 7)
-        both(V, 4)
+        opposite(KT, 1)
+        neighbours(V, 1)
         early, middle, late = range(2), range(2, 3), range(3, 4)
         v = stacked(V, early)
         acc_p[...] = product(p_ref, early, v)
         acc_w[...] = product(w_ref, early, v)
-        both(VT, 2)
+        neighbours(VT, 0)
         top = jnp.maximum(mx[...], jnp.max(mx_late[...], axis=1, keepdims=True) * scale2)
         factor = jnp.exp2(mx[...] - top)
         alpha[...] = factor
@@ -383,22 +398,23 @@
         lsum[...] = lsum[...] * factor
         gsum[...] = gsum[...] * factor
         weights(3, mx)
-        both(VT, 4)
+        neighbours(VT, 1)
         v = stacked(V, middle)
         acc_p[...] += product(p_ref, middle, v)
         acc_w[...] += product(w_ref, middle, v)
-        take(V, 6)
+        opposite(V, 0)
         acc_t[...] = product(p_ref, early, stacked(VT, early))
-        take(V, 7)
+        opposite(V, 1)
         acc_t[...] += product(p_ref, middle, stacked(VT, middle))
         v = stacked(V, late)
         inverse = 1.0 / jnp.sum(lsum[...], axis=1, keepdims=True)
         slope = jnp.sum(gsum[...], axis=1, keepdims=True) * inverse * scale
         attended = (acc_p[...] * alpha[...] + product(p_ref, late, v)) * inverse
         outsend[0] = attended.astype(jnp.bfloat16).reshape(Y * Z, ROWS, HD)
-        both(VT, 6)
         give(0, 1)
         give(0, 0)
+        opposite(VT, 0)
+        opposite(VT, 1)
         acc_w[...] = (acc_w[...] * alpha[...] + product(w_ref, late, v)) * (
             inverse * scale
         ) - slope * attended
@@ -413,6 +429,17 @@
             ).reshape(Y * near, ROWS, HD)
             give(1, u)
 
+    @pl.when(jnp.logical_not(computes))
+    def _():
+        for r, a in enumerate(RELAYED):
+            for j in range(J):
+                part = passing.at[r, j]
+                pltpu.make_async_copy(part, part, psem.at[r, j]).wait()
+                pltpu.make_async_remote_copy(
+                    src_ref=part, dst_ref=kv.at[a, own + 1], send_sem=psend,
+                    recv_sem=rsem.at[RING.index(a), 3], device_id=device(across_x, j, z, c),
+                ).start()
+
     for which, out in ((0, o_out), (1, ot_out)):
         pltpu.make_async_copy(out, out, osem.at[which]).wait()
 
@@ -436,6 +463,7 @@
     @pl.when(jnp.logical_not(computes))
     def _():
         sent(heads)
+        arrived(psend, len(RELAYED) * J)
 
 
 def shards(queries, key_vectors, values, query_tangent, key_tangent, value_tangent,
@@ -470,16 +498,19 @@
             pltpu.VMEM((rows, HD), jnp.float32),
             pltpu.VMEM((rows, HD), jnp.float32),
             pltpu.VMEM((2, Y * Z, ROWS, HD), jnp.bfloat16),
+            pltpu.VMEM((len(RELAYED), J, Y, span // 2, HD), jnp.bfloat16),
             pltpu.SemaphoreType.DMA((2,)),
             pltpu.SemaphoreType.DMA((6,)),
             pltpu.SemaphoreType.DMA((5, 2)),
-            pltpu.SemaphoreType.DMA((4, 10)),
-            pltpu.SemaphoreType.DMA((4, 8)),
+            pltpu.SemaphoreType.DMA((4, 4)),
+            pltpu.SemaphoreType.DMA((4, 4)),
             pltpu.SemaphoreType.DMA((5,)),
             pltpu.SemaphoreType.DMA((4,)),
             pltpu.SemaphoreType.DMA((4,)),
             pltpu.SemaphoreType.DMA((2,)),
             pltpu.SemaphoreType.DMA((2,)),
+            pltpu.SemaphoreType.DMA((len(RELAYED), J)),
+            pltpu.SemaphoreType.DMA,
         ],
         compiler_params=pltpu.CompilerParams(
             collective_id=0, has_side_effects=True, vmem_limit_bytes=54975 * 1024

time: 52.3 us -> 50.4 us (0.964)
  Pallas kernels: 49.6 us -> 47.7 us
    pallas_call x1, Pallas kernels: 49.6 us -> 47.7 us  [shards(): pl.pallas_call(kernel, out_shape=(out, out), in_specs=[hbm] * 8, out_spec...]
where the time goes in v7:
time: 50.4 us; the launch traced here: 50.3 us
  Pallas kernels  47.7 us (95%)
  between operations  1.32 us (3%)
  local copies, waits for them, and re-layouts  1.29 us (3%)
    pallas_call x1, Pallas kernels, shards(): pl.pallas_call(kernel, out_shape=(out, out), in_specs=[hbm] * 8, out_spec...  47.7 us
    unnamed x4, local copies, waits for them, and re-layouts  1.29 us

profile of v7, /device:TPU:1, one launch (start us, length us, event | category | flops | bytes accessed | tf_op | source)
XLA Modules:
  0.0 50.3 jit_solution(6965146416813092717)
XLA Ops:
  0.6 0.0 copy-start
  1.3 0.0 copy-done
  1.3 47.7 %shard_map.95 = (bf16[16,3072]{1,0:T(8,128)(2,1)S(1)}, bf16[16,3072]{1,0:T(8,128)(2,1)S(1)}) custom-call(bf16[16,3072]{1,0:T(8,128)(2,1)} %q_in.1, bf16[16,3072]{1,0:T(8,128)(2,1)} %k_in.1, bf16[16,3072]{1,0:T(8,128)(2,1)} %v_in.1, bf16[16,3072]{1,0:T(8,128)(2,1)} %qt_in.1, bf16[16,3072]{1,0:T(8,128)(2,1)} %kt_in.1, bf16[16,3072]{1,0:T(8,128)(2,1)} %vt_in.1, ...), custom_call_target="tpu_custom_call" | custom-call | tf_op jit(solution)/shard_map/pallas_call | solution.py:478
  49.0 0.6 %copy.13 = bf16[16,3072]{1,0:T(8,128)(2,1)} copy(bf16[16,3072]{1,0:T(8,128)(2,1)S(1)} %get-tuple-element.4) | data formatting | bytes 196608
  49.7 0.6 %copy.14 = bf16[16,3072]{1,0:T(8,128)(2,1)} copy(bf16[16,3072]{1,0:T(8,128)(2,1)S(1)} %get-tuple-element.5) | data formatting | bytes 196608
Async XLA Ops:
  0.6 0.7 %copy-start = (s32[128]{0:T(128)S(1)}, s32[128]{0:T(128)}, u32[]{:S(2)}) copy-start(s32[128]{0:T(128)} %frame_in.1) | copy-start | bytes 1540

commit v8 on v7

--- a/solution.py
+++ b/solution.py
@@ -374,16 +374,13 @@
         mx[...] = jnp.broadcast_to(jnp.max(mx[...], axis=1, keepdims=True) * scale2, mx.shape)
         opposite(K, 1)
 
-        def second():
-            start(VT, 0)
-            opposite(KT, 0)
-
-        def third():
-            start(VT, 1)
-            neighbours(V, 0)
-
-        loop(lambda j: weights(j, mx), 0, 3, {1: second, 2: third})
+        loop(lambda j: weights(j, mx), 0, 3, {
+            1: lambda: start(VT, 0),
+            2: lambda: start(VT, 1),
+        })
+        opposite(KT, 0)
         scores(3, mx_late)
+        neighbours(V, 0)
         opposite(KT, 1)
         neighbours(V, 1)
         early, middle, late = range(2), range(2, 3), range(3, 4)
@@ -440,9 +437,6 @@
                     recv_sem=rsem.at[RING.index(a), 3], device_id=device(across_x, j, z, c),
                 ).start()
 
-    for which, out in ((0, o_out), (1, ot_out)):
-        pltpu.make_async_copy(out, out, osem.at[which]).wait()
-
     def sent(count):
         for g, (first, arrays) in enumerate(GROUPS):
             part = send.at[pl.ds(0, count), pl.ds(first, arrays)]
@@ -464,6 +458,9 @@
     def _():
         sent(heads)
         arrived(psend, len(RELAYED) * J)
+
+    for which, out in ((0, o_out), (1, ot_out)):
+        pltpu.make_async_copy(out, out, osem.at[which]).wait()
 
 
 def shards(queries, key_vectors, values, query_tangent, key_tangent, value_tangent,

time: 50.4 us -> 50.3 us (level)
  no operation moved by 1% of the time
where the time goes in v8:
time: 50.3 us; the launch traced here: 50.1 us
  Pallas kernels  47.5 us (94%)
  between operations  1.32 us (3%)
  local copies, waits for them, and re-layouts  1.29 us (3%)
    pallas_call x1, Pallas kernels, shards(): pl.pallas_call(kernel, out_shape=(out, out), in_specs=[hbm] * 8, out_spec...  47.5 us
    unnamed x4, local copies, waits for them, and re-layouts  1.29 us

profile of v8, /device:TPU:1, one launch (start us, length us, event | category | flops | bytes accessed | tf_op | source)
XLA Modules:
  0.0 50.1 jit_solution(1838504287611895641)
XLA Ops:
  0.6 0.0 copy-start
  1.3 0.0 copy-done
  1.3 47.5 %shard_map.95 = (bf16[16,3072]{1,0:T(8,128)(2,1)S(1)}, bf16[16,3072]{1,0:T(8,128)(2,1)S(1)}) custom-call(bf16[16,3072]{1,0:T(8,128)(2,1)} %q_in.1, bf16[16,3072]{1,0:T(8,128)(2,1)} %k_in.1, bf16[16,3072]{1,0:T(8,128)(2,1)} %v_in.1, bf16[16,3072]{1,0:T(8,128)(2,1)} %qt_in.1, bf16[16,3072]{1,0:T(8,128)(2,1)} %kt_in.1, bf16[16,3072]{1,0:T(8,128)(2,1)} %vt_in.1, ...), custom_call_target="tpu_custom_call" | custom-call | tf_op jit(solution)/shard_map/pallas_call | solution.py:475
  48.9 0.6 %copy.13 = bf16[16,3072]{1,0:T(8,128)(2,1)} copy(bf16[16,3072]{1,0:T(8,128)(2,1)S(1)} %get-tuple-element.4) | data formatting | bytes 196608
  49.5 0.6 %copy.14 = bf16[16,3072]{1,0:T(8,128)(2,1)} copy(bf16[16,3072]{1,0:T(8,128)(2,1)S(1)} %get-tuple-element.5) | data formatting | bytes 196608
Async XLA Ops:
  0.6 0.7 %copy-start = (s32[128]{0:T(128)S(1)}, s32[128]{0:T(128)}, u32[]{:S(2)}) copy-start(s32[128]{0:T(128)} %frame_in.1) | copy-start | bytes 1540

commit v9 on v7

--- a/solution.py
+++ b/solution.py
@@ -412,9 +412,9 @@
         attended = (acc_p[...] * alpha[...] + product(p_ref, late, v)) * inverse
         outsend[0] = attended.astype(jnp.bfloat16).reshape(Y * Z, ROWS, HD)
         give(0, 1)
-        give(0, 0)
         opposite(VT, 0)
         opposite(VT, 1)
+        give(0, 0)
         acc_w[...] = (acc_w[...] * alpha[...] + product(w_ref, late, v)) * (
             inverse * scale
         ) - slope * attended

time: 50.4 us -> 50.4 us (level)
  no operation moved by 1% of the time
where the time goes in v9:
time: 50.4 us; the launch traced here: 50.3 us
  Pallas kernels  47.7 us (95%)
  between operations  1.32 us (3%)
  local copies, waits for them, and re-layouts  1.29 us (3%)
    pallas_call x1, Pallas kernels, shards(): pl.pallas_call(kernel, out_shape=(out, out), in_specs=[hbm] * 8, out_spec...  47.7 us
    unnamed x4, local copies, waits for them, and re-layouts  1.29 us

profile of v9, /device:TPU:1, one launch (start us, length us, event | category | flops | bytes accessed | tf_op | source)
XLA Modules:
  0.0 50.3 jit_solution(1976680988308832529)
XLA Ops:
  0.6 0.0 copy-start
  1.3 0.0 copy-done
  1.3 47.7 %shard_map.95 = (bf16[16,3072]{1,0:T(8,128)(2,1)S(1)}, bf16[16,3072]{1,0:T(8,128)(2,1)S(1)}) custom-call(bf16[16,3072]{1,0:T(8,128)(2,1)} %q_in.1, bf16[16,3072]{1,0:T(8,128)(2,1)} %k_in.1, bf16[16,3072]{1,0:T(8,128)(2,1)} %v_in.1, bf16[16,3072]{1,0:T(8,128)(2,1)} %qt_in.1, bf16[16,3072]{1,0:T(8,128)(2,1)} %kt_in.1, bf16[16,3072]{1,0:T(8,128)(2,1)} %vt_in.1, ...), custom_call_target="tpu_custom_call" | custom-call | tf_op jit(solution)/shard_map/pallas_call | solution.py:478
  49.0 0.6 %copy.13 = bf16[16,3072]{1,0:T(8,128)(2,1)} copy(bf16[16,3072]{1,0:T(8,128)(2,1)S(1)} %get-tuple-element.4) | data formatting | bytes 196608
  49.7 0.6 %copy.14 = bf16[16,3072]{1,0:T(8,128)(2,1)} copy(bf16[16,3072]{1,0:T(8,128)(2,1)S(1)} %get-tuple-element.5) | data formatting | bytes 196608
Async XLA Ops:
  0.6 0.7 %copy-start = (s32[128]{0:T(128)S(1)}, s32[128]{0:T(128)}, u32[]{:S(2)}) copy-start(s32[128]{0:T(128)} %frame_in.1) | copy-start | bytes 1540
